TPU v7x, 32 devices: a whole 2x2x4 slice. The times are simulated.
32 devices in a mesh: seq: 4 (over y, x), batch: 8 (over z, core).
Axes of the slice: x: 2, y: 2, z: 4, core: 2. Of those that a mesh axis runs over, the one named last changes fastest.
Arguments:
- inputs: bfloat16 [8, 8192, 512], P('batch', 'seq'), may hold values from -6 to 6
- cotangent: bfloat16 [8, 8192, 512], P('batch', 'seq'), may hold values from -6 to 6
- short_lengths: int32 [4, 4], replicated, may hold values from 1 to 3072, 8192 in all within a row
- long_lengths: int32 [4, 2], replicated, may hold values from 1 to 7680, 8192 in all within a row
- norm_gain: float32 [512], replicated, may hold values from 0.1 to 1.9
- w_gates: bfloat16 [512, 3072], replicated, may hold values from -0.25 to 0.25
- gate_bias: float32 [3072], replicated, may hold values from -12 to 4, as said below
- w_out: bfloat16 [1024, 512], replicated, may hold values from -0.1875 to 0.1875
- out_bias: float32 [512], replicated, may hold values from -3 to 3
- mlp_gain: float32 [512], replicated, may hold values from 0.1 to 1.9
- w_up: bfloat16 [512, 2048], replicated, may hold values from -0.25 to 0.25
- up_bias: float32 [2048], replicated, may hold values from -3 to 3
- w_down: bfloat16 [2048, 512], replicated, may hold values from -0.125 to 0.125
- down_bias: float32 [512], replicated, may hold values from -3 to 3
Outputs:
- result: bfloat16 [8, 8192, 512], P('batch', 'seq')
- grad_input: float32 [8, 8192, 512], P('batch', 'seq')
- grad_norm_gain: float32 [512], replicated
- grad_w_gates: float32 [512, 3072], replicated
- grad_gate_bias: float32 [3072], replicated
- grad_w_out: float32 [1024, 512], replicated
- grad_out_bias: float32 [512], replicated
- grad_mlp_gain: float32 [512], replicated
- grad_w_up: float32 [512, 2048], replicated
- grad_up_bias: float32 [2048], replicated
- grad_w_down: float32 [2048, 512], replicated
- grad_down_bias: float32 [512], replicated
Inputs may be any that keep to these rules, and one draw needn't show every extreme that they name: `short_lengths`: row g gives, in order, the lengths of the 4 sequences that fill the 8192 tokens of group g. `long_lengths`: row g gives, in order, the lengths of the two sequences that fill the 8192 tokens of group 4 + g. `gate_bias`: three blocks of 1024: forget biases, input biases, candidate biases.
All inputs are finite; a program needn't handle non-finite values.
Results may differ from a plain program's by a relative error of at most 0.0068.
Values sent between devices are 32-bit elements; how exact they have to be, the bound alone decides.
A program may use at most 256 MiB of HBM per device.

v0:
```python
import math

import jax
import jax.numpy as jnp
from jax import lax
from jax.sharding import PartitionSpec as P

epsilon = 1e-06


def prefix(x, axis, combine, identity, reverse):
    devices, position = (lax.axis_size(axis), lax.axis_index(axis))
    everything = jax.tree.map(lambda part: lax.all_gather(part, axis), x)
    start = jax.tree.map(
        lambda part, zero: jnp.broadcast_to(jnp.asarray(zero, part.dtype), part.shape), x, identity
    )

    def lap(k, before):
        at = devices - 1 - k if reverse else k
        reached = at > position if reverse else at < position
        new = combine(before, jax.tree.map(lambda part: part[at], everything))
        return jax.tree.map(lambda a, b: jnp.where(reached, a, b), new, before)

    return lax.fori_loop(0, devices, lap, start)


def combine(earlier, later):
    return (earlier[0] * later[0], later[0] * earlier[1] + later[1])


def block_scan(first, second, reverse):
    total_rows, width = first.shape
    inner_rows = math.gcd(total_rows, 16)
    outer_rows = total_rows // inner_rows
    decay_blocks = first.reshape(outer_rows, inner_rows, width)
    drive_blocks = second.reshape(outer_rows, inner_rows, width)
    cum_list = [None] * inner_rows
    state_list = [None] * inner_rows
    order = range(inner_rows - 1, -1, -1) if reverse else range(inner_rows)
    run_decay = None
    run_state = None
    for place in order:
        step_decay = decay_blocks[:, place]
        step_drive = drive_blocks[:, place]
        if run_decay is None:
            run_decay, run_state = (step_decay, step_drive)
        else:
            run_decay, run_state = combine((run_decay, run_state), (step_decay, step_drive))
        cum_list[place] = run_decay
        state_list[place] = run_state
    cum_local = jnp.stack(cum_list, axis=1)
    state_local = jnp.stack(state_list, axis=1)
    incl_decay, incl_state = lax.associative_scan(
        combine, (run_decay, run_state), axis=0, reverse=reverse
    )
    ones_rows = jnp.ones((1, width), jnp.float32)
    zeros_rows = jnp.zeros((1, width), jnp.float32)
    if reverse:
        prev_decay = jnp.concatenate([incl_decay[1:], ones_rows], axis=0)
        prev_state = jnp.concatenate([incl_state[1:], zeros_rows], axis=0)
    else:
        prev_decay = jnp.concatenate([ones_rows, incl_decay[:-1]], axis=0)
        prev_state = jnp.concatenate([zeros_rows, incl_state[:-1]], axis=0)
    full_state = state_local + cum_local * prev_state[:, None, :]
    full_cum = cum_local * prev_decay[:, None, :]
    return (full_cum.reshape(total_rows, width), full_state.reshape(total_rows, width))


def normalize(values, gain_vec):
    inv_scale = lax.rsqrt(jnp.mean(values * values, axis=-1, keepdims=True) + epsilon)
    return (values * inv_scale * gain_vec, inv_scale)


def norm_back(values, inv_scale, gain_vec, incoming_grad):
    weighted = incoming_grad * gain_vec
    grad_gain = jnp.sum(incoming_grad * values * inv_scale, axis=0)
    grad_values = inv_scale * weighted - values * inv_scale**3 * jnp.mean(
        weighted * values, axis=-1, keepdims=True
    )
    return (grad_values, grad_gain)


def gate_terms(mixed_in, keep_mask):
    width = mixed_in.shape[-1] // 3
    forget = jax.nn.sigmoid(mixed_in[:, :width])
    inputs_gate = jax.nn.sigmoid(mixed_in[:, width : 2 * width])
    candidate = mixed_in[:, 2 * width :]
    totals = forget + inputs_gate
    return (forget / totals * keep_mask, inputs_gate / totals * candidate)


def exact_gelu(values):
    return jax.nn.gelu(values, approximate=False)


def outer_sum(left, right):
    return lax.dot_general(
        left, right, (((0,), (0,)), ((), ())), preferred_element_type=jnp.float32
    )


def times_transposed(left, right):
    return lax.dot_general(
        left, right, (((1,), (1,)), ((), ())), preferred_element_type=jnp.float32
    )


def starts_of(lengths_row, position):
    starts = jnp.cumsum(lengths_row) - lengths_row
    return jnp.any(position[:, None] == starts[None, :], axis=1)


def per_device(
    inputs,
    cotangent,
    short_lengths,
    long_lengths,
    norm_gain,
    w_gates,
    gate_bias,
    w_out,
    out_bias,
    mlp_gain,
    w_up,
    up_bias,
    w_down,
    down_bias,
):
    tok_rows = inputs.shape[1]
    source = inputs[0].astype(jnp.float32)
    grad_result = cotangent[0]
    group_index = lax.axis_index("batch")
    half_groups = short_lengths.shape[0]
    short_row = lax.dynamic_index_in_dim(
        short_lengths, jnp.clip(group_index, 0, half_groups - 1), 0, keepdims=False
    )
    long_row = lax.dynamic_index_in_dim(
        long_lengths, jnp.clip(group_index - half_groups, 0, half_groups - 1), 0, keepdims=False
    )
    position = lax.axis_index("seq") * tok_rows + jnp.arange(tok_rows, dtype=jnp.int32)
    starting = jnp.where(
        group_index < half_groups, starts_of(short_row, position), starts_of(long_row, position)
    )
    keep_mask = (1.0 - starting.astype(jnp.float32))[:, None]
    normed, scale_one = normalize(source, norm_gain)
    normed_low = normed.astype(jnp.bfloat16)
    mixed_in = jnp.dot(normed_low, w_gates, preferred_element_type=jnp.float32) + gate_bias
    (decays, drives), gate_back = jax.vjp(lambda values: gate_terms(values, keep_mask), mixed_in)
    width = decays.shape[1]
    ones_row = jnp.ones((width,), jnp.float32)
    zeros_row = jnp.zeros((width,), jnp.float32)
    cum_decay, state_local = block_scan(decays, drives, False)
    unused, incoming = prefix(
        (cum_decay[-1], state_local[-1]), "seq", combine, (ones_row, zeros_row), False
    )
    states = state_local + cum_decay * incoming
    states_low = states.astype(jnp.bfloat16)
    resid = source + jnp.dot(states_low, w_out, preferred_element_type=jnp.float32) + out_bias
    normed_two, scale_two = normalize(resid, mlp_gain)
    normed_two_low = normed_two.astype(jnp.bfloat16)
    upper_in = jnp.dot(normed_two_low, w_up, preferred_element_type=jnp.float32) + up_bias
    active, gelu_back = jax.vjp(exact_gelu, upper_in)
    active_low = active.astype(jnp.bfloat16)
    result = resid + jnp.dot(active_low, w_down, preferred_element_type=jnp.float32) + down_bias
    grad_w_down = outer_sum(active_low, grad_result)
    grad_down_bias = jnp.sum(grad_result.astype(jnp.float32), axis=0)
    grad_active = times_transposed(grad_result, w_down)
    grad_upper = gelu_back(grad_active)[0].astype(jnp.bfloat16)
    grad_w_up = outer_sum(normed_two_low, grad_upper)
    grad_up_bias = jnp.sum(grad_upper.astype(jnp.float32), axis=0)
    grad_normed_two = times_transposed(grad_upper, w_up)
    grad_resid_norm, grad_mlp_gain = norm_back(resid, scale_two, mlp_gain, grad_normed_two)
    grad_resid = grad_result.astype(jnp.float32) + grad_resid_norm
    grad_resid_low = grad_resid.astype(jnp.bfloat16)
    grad_w_out = outer_sum(states_low, grad_resid_low)
    grad_out_bias = jnp.sum(grad_resid_low.astype(jnp.float32), axis=0)
    grad_states = times_transposed(grad_resid_low, w_out)
    cum_again, local_again = block_scan(decays, drives, False)
    unused_again, incoming_used = prefix(
        (cum_again[-1], local_again[-1]), "seq", combine, (ones_row, zeros_row), False
    )
    states_used = local_again + cum_again * incoming_used
    next_decay = jnp.concatenate([decays[1:], jnp.ones((1, width), jnp.float32)], axis=0)
    cum_next, lambda_local = block_scan(next_decay, grad_states, True)
    first_total = decays[0] * cum_next[0]
    first_term = decays[0] * lambda_local[0]
    unused_back, entering = prefix(
        (first_total, first_term), "seq", combine, (ones_row, zeros_row), True
    )
    lambdas = lambda_local + cum_next * entering
    previous = jnp.concatenate([incoming_used[None, :], states_used[:-1]], axis=0)
    grad_mixed = gate_back((lambdas * previous, lambdas))[0].astype(jnp.bfloat16)
    grad_w_gates = outer_sum(normed_low, grad_mixed)
    grad_gate_bias = jnp.sum(grad_mixed.astype(jnp.float32), axis=0)
    grad_normed = times_transposed(grad_mixed, w_gates)
    grad_source_norm, grad_norm_gain = norm_back(source, scale_one, norm_gain, grad_normed)
    grad_input = grad_resid + grad_source_norm
    summed = lax.psum(
        (
            grad_norm_gain,
            grad_w_gates,
            grad_gate_bias,
            grad_w_out,
            grad_out_bias,
            grad_mlp_gain,
            grad_w_up,
            grad_up_bias,
            grad_w_down,
            grad_down_bias,
        ),
        ("seq", "batch"),
    )
    return (
        result.astype(jnp.bfloat16)[None],
        grad_input[None],
        summed[0],
        summed[1],
        summed[2],
        summed[3],
        summed[4],
        summed[5],
        summed[6],
        summed[7],
        summed[8],
        summed[9],
    )


def solution(mesh):
    in_specs = (
        P("batch", "seq", None),
        P("batch", "seq", None),
        P(),
        P(),
        P(),
        P(),
        P(),
        P(),
        P(),
        P(),
        P(),
        P(),
        P(),
        P(),
    )
    out_specs = (
        P("batch", "seq", None),
        P("batch", "seq", None),
        P(),
        P(),
        P(),
        P(),
        P(),
        P(),
        P(),
        P(),
        P(),
        P(),
    )
    return jax.shard_map(
        per_device, mesh=mesh, in_specs=in_specs, out_specs=out_specs, check_vma=False
    )
```

profile of v0, /device:TPU:0, one launch (start us, length us, event | category | flops | bytes accessed | tf_op | source)
XLA Modules:
  0.0 1121.7 jit_solution(14050799920988187729)
XLA Ops:
  14.1 13.6 %broadcast_add_fusion = f32[2048,3072]{1,0:T(8,128)} fusion(f32[3072]{0:T(1024)} %param.24, bf16[512,3072]{1,0:T(8,128)(2,1)S(1)} %copy-done, bf16[1,2048,512]{2,1,0:T(8,128)(2,1)} %param.18, f32[512]{0:T(512)} %param.22, f32[2048]{0:T(1024)S(1)} %get-tuple-element.520), kind=kOutput, calls=%fused_computation.28 | convolution fusion | flops 6452936704 | bytes 30431232 | tf_op jit(solution)/shard_map/dot_general | solution.py:147
  27.7 14.2 %slice_multiply_fusion.1 = (f32[2048,1024]{1,0:T(8,128)}, f32[2048,1024]{1,0:T(8,128)S(1)}) fusion(f32[2048,3072]{1,0:T(8,128)} %broadcast_add_fusion), kind=kLoop, calls=%fused_computation.53 | loop fusion | flops 20971520 | bytes 41943040 | tf_op jit(solution)/shard_map/jvp()/mul | solution.py:89
  41.9 9.7 divide_multiply_fusion
  51.6 8.7 slice.1056
  60.3 8.4 concatenate.118
  68.7 31.5 %fusion.97 = (f32[128,1,1024]{2,1,0:T(1,128)}, f32[128,1,1024]{2,1,0:T(1,128)}, f32[128,1,1024]{2,1,0:T(1,128)}, f32[128,1,1024]{2,1,0:T(1,128)}, f32[128,1,1024...) fusion(f32[128,16,1024]{2,1,0:T(8,128)} %bitcast.253), kind=kLoop, calls=%fused_computation.343 | loop fusion | bytes 16777216 | tf_op jit(solution)/shard_map/slice | solution.py:43
  113.8 30.3 %fusion.99 = (f32[128,1,1024]{2,1,0:T(1,128)}, f32[128,1,1024]{2,1,0:T(1,128)S(1)}, f32[128,1,1024]{2,1,0:T(1,128)S(1)}, f32[128,1,1024]{2,1,0:T(1,128)S(1)}, f3...) fusion(f32[128,16,1024]{2,1,0:T(8,128)} %bitcast.242), kind=kLoop, calls=%fused_computation.345 | loop fusion | bytes 16777216 | tf_op jit(solution)/shard_map/slice | solution.py:43
  159.4 30.4 %fusion.98 = (f32[128,1,1024]{2,1,0:T(1,128)}, f32[128,1,1024]{2,1,0:T(1,128)}, f32[128,1,1024]{2,1,0:T(1,128)}, f32[128,1,1024]{2,1,0:T(1,128)}, f32[128,1,1024...) fusion(f32[128,16,1024]{2,1,0:T(8,128)} %bitcast.244), kind=kLoop, calls=%fused_computation.344 | loop fusion | bytes 16777216 | tf_op jit(solution)/shard_map/slice | solution.py:44
  194.9 8.2 bitcast_add_fusion
  329.0 24.1 %stack.9 = f32[128,16,1024]{2,1,0:T(8,128)} concatenate(f32[128,1,1024]{2,1,0:T(1,128)} %get-tuple-element.456, f32[128,1,1024]{2,1,0:T(1,128)} %copy.469, f32[128,1,1024]{2,1,0:T(1,128)} %copy.470, f32[128,1,1024]{2,1,0:T(1,128)} %copy.471, f32[128,1,1024]{2,1,0:T(1,128)} %copy.472, f32[128,1,1024]{2,1,0:T(1,128)} %copy.473, f32[128,1,1024]{2,1,0:T(1,128)} %copy.474, ...), dimensions={1} | concatenate | bytes 16777216 | tf_op jit(solution)/shard_map/stack | solution.py:51
  353.1 24.1 %stack.8 = f32[128,16,1024]{2,1,0:T(8,128)} concatenate(f32[128,1,1024]{2,1,0:T(1,128)} %get-tuple-element.439, f32[128,1,1024]{2,1,0:T(1,128)} %copy.454, f32[128,1,1024]{2,1,0:T(1,128)} %copy.455, f32[128,1,1024]{2,1,0:T(1,128)} %copy.456, f32[128,1,1024]{2,1,0:T(1,128)} %copy.457, f32[128,1,1024]{2,1,0:T(1,128)} %copy.458, f32[128,1,1024]{2,1,0:T(1,128)} %copy.459, ...), dimensions={1} | concatenate | bytes 16777216 | tf_op jit(solution)/shard_map/stack | solution.py:52
  377.2 10.1 multiply_add_fusion.3
  390.5 9.6 all-gather.1
  400.1 8.1 all-gather
  408.5 12.3 %multiply_add_fusion.2 = f32[2048,1024]{1,0:T(8,128)} fusion(f32[1024]{0:T(1024)S(1)} %get-tuple-element.250, f32[128,16,1024]{2,1,0:T(8,128)} %get-tuple-element.425, f32[128,16,1024]{2,1,0:T(8,128)} %copy-done.5), kind=kLoop, calls=%fused_computation.48 | loop fusion | flops 4194304 | bytes 25169920 | tf_op jit(solution)/shard_map/add | solution.py:156
  428.1 43.8 %multiply_convert_fusion = (bf16[2048,2048]{1,0:T(8,128)(2,1)}, f32[2048,2048]{1,0:T(8,128)}, f32[2048,2048]{1,0:T(8,128)}) fusion(f32[2048]{0:T(1024)S(1)} %copy-done.125, bf16[512,2048]{1,0:T(8,128)(2,1)S(1)} %copy-done.122, f32[2048,512]{1,0:T(8,128)S(1)} %get-tuple-element.536, f32[512]{0:T(512)S(1)} %copy-done.119, f32[2048]{0:T(1024)S(1)} %get-tuple-element.528), kind=kOutput, calls=%fused_computation.12 | convolution fusion | flops 4574937088 | bytes 48252928 | tf_op jit(solution)/shard_map/dot_general | solution.py:161
  471.9 22.5 %convert_reduce_fusion.1 = (f32[2048]{0:T(1024)}, bf16[2048,2048]{1,0:T(8,128)(2,1)}) fusion(f32[2048,2048]{1,0:T(8,128)} %get-tuple-element.347, bf16[2048,512]{1,0:T(8,128)(2,1)} %param.30, bf16[1,2048,512]{2,1,0:T(8,128)(2,1)} %param.19, f32[2048,2048]{1,0:T(8,128)} %get-tuple-element.537, f32[2048]{0:T(1024)S(1)} %copy-done.125), kind=kOutput, calls=%fused_computation.10 | convolution fusion | flops 4366268416 | bytes 46153728 | tf_op jit(solution)/shard_map/dot_general | solution.py:103
  494.4 11.5 %fusion.90 = f32[512,2048]{1,0:T(8,128)} fusion(bf16[2048,2048]{1,0:T(8,128)(2,1)} %get-tuple-element.541, f32[2048,512]{1,0:T(8,128)} %copy-done.64, f32[512]{0:T(512)S(1)} %copy-done.119, f32[2048]{0:T(1024)S(1)} %get-tuple-element.528), kind=kOutput, calls=%fused_computation.338 | convolution fusion | flops 4298113024 | bytes 16787456 | tf_op jit(solution)/shard_map/dot_general | solution.py:97
  505.9 8.2 multiply_reduce_fusion
  526.1 30.4 %fusion.96 = (f32[128,1,1024]{2,1,0:T(1,128)}, f32[128,1,1024]{2,1,0:T(1,128)}, f32[128,1,1024]{2,1,0:T(1,128)}, f32[128,1,1024]{2,1,0:T(1,128)}, f32[128,1,1024...) fusion(f32[128,16,1024]{2,1,0:T(8,128)} %bitcast.243), kind=kLoop, calls=%fused_computation.342 | loop fusion | bytes 16777216 | tf_op jit(solution)/shard_map/slice | solution.py:44
  616.9 10.8 fusion.27
  712.8 9.6 multiply_add_fusion.1
  727.3 11.3 %copy.517 = f32[128,16,1024]{2,1,0:T(8,128)S(1)} copy(f32[128,16,1024]{2,0,1:T(8,128)} %get-tuple-element.391) | data formatting | bytes 16777216 | tf_op jit(solution)/shard_map/mul | solution.py:65
  749.1 8.2 all-gather.2
  757.8 19.1 %fusion.92 = (f32[2048,1024]{1,0:T(8,128)}, f32[2048,1024]{1,0:T(8,128)}) fusion(f32[2048,1024]{1,0:T(8,128)} %copy-done.1, f32[2048,3072]{1,0:T(8,128)} %broadcast_add_fusion, f32[1024]{0:T(1024)S(1)} %get-tuple-element.251, f32[128,16,1024]{2,1,0:T(8,128)} %copy-done.4, f32[128,16,1024]{2,1,0:T(8,128)} %copy-done.3), kind=kLoop, calls=%fused_computation.340 | loop fusion | flops 14680064 | bytes 50335744 | tf_op jit(solution)/shard_map/transpose(jvp())/mul | solution.py:89
  776.9 21.3 %fusion.6 = (f32[2048,1024]{1,0:T(8,128)S(1)}, f32[2048,1024]{1,0:T(8,128)}) fusion(f32[2048,1024]{1,0:T(8,128)} %copy-done.1, f32[2048,1024]{1,0:T(8,128)} %get-tuple-element.327, f32[2048,3072]{1,0:T(8,128)} %broadcast_add_fusion, f32[2048]{0:T(1024)S(1)} %copy-done.107, f32[2047,1024]{1,0:T(8,128)} %bitcast.250, f32[1,1024]{1,0:T(1,128)S(1)} %bitcast.258), kind=kLoop, calls=%fused_computation.35 | loop fusion | flops 60817408 | bytes 67117056 | tf_op jit(solution)/shard_map/transpose(jvp())/mul | solution.py:86
  798.2 10.0 convert_reduce_fusion
  808.2 11.8 %fusion.33 = f32[512,3072]{1,0:T(8,128)} fusion(bf16[2048,3072]{1,0:T(8,128)(2,1)} %get-tuple-element.325, bf16[1,2048,512]{2,1,0:T(8,128)(2,1)S(1)} %copy-done.31, f32[512]{0:T(512)S(1)} %copy-done.120, f32[2048]{0:T(1024)S(1)} %copy-done.110), kind=kOutput, calls=%fused_computation.84 | convolution fusion | flops 6446645248 | bytes 20981760 | tf_op jit(solution)/shard_map/dot_general | solution.py:97
  820.0 11.8 %fusion.25 = (f32[512]{0:T(512)S(1)}, f32[2048]{0:T(1024)S(1)}, f32[2048,512]{1,0:T(8,128)}) fusion(bf16[1,2048,512]{2,1,0:T(8,128)(2,1)} %param.18, f32[2048]{0:T(1024)S(1)} %copy-done.110, f32[512]{0:T(512)S(1)} %copy-done.120, bf16[2048,3072]{1,0:T(8,128)(2,1)} %get-tuple-element.325, bf16[512,3072]{1,0:T(8,128)(2,1)S(1)} %copy-done), kind=kOutput, calls=%fused_computation.68 | convolution fusion | flops 6449788416 | bytes 22040576 | tf_op jit(solution)/shard_map/dot_general | solution.py:103
  831.9 42.3 %all-reduce.64 = (f32[512]{0:T(512)}, f32[3072]{0:T(1024)}, f32[512]{0:T(512)}, f32[512]{0:T(512)}, f32[2048]{0:T(1024)}, /*index=5*/f32[512]{0:T(512)}) all-reduce(f32[512]{0:T(512)S(1)} %get-tuple-element.290, f32[3072]{0:T(1024)S(1)} %get-tuple-element.324, ...), channel_id=1, replica_groups=mesh['seq'=4,'batch'=8] {'seq','batch'}, use_global_device_ids=true, to_apply=%region_13.14 | all-reduce | flops 7168 | bytes 57344 | tf_op jit(solution)/shard_map/psum | solution.py:198
  881.9 9.5 fusion.26
  891.4 210.1 %all-reduce.68.cloned.1.call-done = (f32[512,3072]{1,0:T(8,128)}, f32[1024,512]{1,0:T(8,128)}, f32[512,2048]{1,0:T(8,128)}, f32[2048,512]{1,0:T(8,128)}) async-done(((f32[512,3072]{1,0:T(8,128)}, f32[1024,512]{1,0:T(8,128)}, f32[512,2048]{1,0:T(8,128)}, f32[2048,512]{1,0:T(8,128)}), (f32[512,3072]{1,0:T(8,128)}, f32[1024,512]{1,0:T(8,128)}, f32[512,2048]{1,0:T(8,128)}, ...) | async-done | bytes 16777232 | tf_op jit(solution)/shard_map/psum | solution.py:198
  (606 shorter events, 370.2 us)
Async XLA Ops:
  7.2 1094.3 %all-reduce.68.cloned.1.call-start = ((), (), s32[]{:S(2)}) async-start(), calls=%async_computation | async-start | bytes 33554432 | tf_op jit(solution)/shard_map/psum | solution.py:198
  159.4 35.5 %copy-start.38 = (f32[128,1,1024]{2,1,0:T(1,128)S(1)}, f32[128,1,1024]{2,1,0:T(1,128)}, u32[]{:S(2)}) copy-start(f32[128,1,1024]{2,1,0:T(1,128)} %copy-done.37) | copy-start | bytes 1572868
  159.4 35.5 %copy-start.40 = (f32[128,1,1024]{2,1,0:T(1,128)S(1)}, f32[128,1,1024]{2,1,0:T(1,128)}, u32[]{:S(2)}) copy-start(f32[128,1,1024]{2,1,0:T(1,128)} %copy-done.39) | copy-start | bytes 1572868
  159.4 35.5 %copy-start.42 = (f32[128,1,1024]{2,1,0:T(1,128)S(1)}, f32[128,1,1024]{2,1,0:T(1,128)}, u32[]{:S(2)}) copy-start(f32[128,1,1024]{2,1,0:T(1,128)} %copy-done.41) | copy-start | bytes 1572868
  228.6 34.5 %copy-start.97 = (f32[15,1024]{1,0:T(8,128)S(1)}, f32[15,1024]{1,0:T(8,128)}, u32[]{:S(2)}) copy-start(f32[15,1024]{1,0:T(8,128)} %slice.844) | copy-start | bytes 184324
  228.6 34.5 %copy-start.98 = (f32[15,1024]{1,0:T(8,128)S(1)}, f32[15,1024]{1,0:T(8,128)}, u32[]{:S(2)}) copy-start(f32[15,1024]{1,0:T(8,128)} %slice.811) | copy-start | bytes 184324
  231.2 28.4 %copy-start.104 = (f32[7,1024]{1,0:T(8,128)S(1)}, f32[7,1024]{1,0:T(8,128)}, u32[]{:S(2)}) copy-start(f32[7,1024]{1,0:T(8,128)} %slice.842) | copy-start | bytes 86020
  231.2 28.4 %copy-start.105 = (f32[7,1024]{1,0:T(8,128)S(1)}, f32[7,1024]{1,0:T(8,128)}, u32[]{:S(2)}) copy-start(f32[7,1024]{1,0:T(8,128)} %slice.817) | copy-start | bytes 86020
  232.5 26.3 %copy-start.115 = (f32[1,1024]{1,0:T(1,128)S(1)}, f32[1,1024]{1,0:T(1,128)}, u32[]{:S(2)}) copy-start(f32[1,1024]{1,0:T(1,128)} %slice.1039) | copy-start | bytes 12292
  232.5 26.3 %copy-start.114 = (f32[1,1024]{1,0:T(1,128)S(1)}, f32[1,1024]{1,0:T(1,128)}, u32[]{:S(2)}) copy-start(f32[1,1024]{1,0:T(1,128)} %slice.1016) | copy-start | bytes 12292
  232.7 21.9 %copy-start.83 = (f32[128,1,1024]{2,0,1:T(8,128)S(1)}, f32[128,1,1024]{2,0,1:T(8,128)}, u32[]{:S(2)}) copy-start(f32[128,1,1024]{2,0,1:T(8,128)} %get-tuple-element.353) | copy-start | bytes 1572868
  297.5 20.8 %copy-start.87 = (f32[128,1,1024]{2,0,1:T(8,128)S(1)}, f32[128,1,1024]{2,0,1:T(8,128)}, u32[]{:S(2)}) copy-start(f32[128,1,1024]{2,0,1:T(8,128)} %get-tuple-element.464) | copy-start | bytes 1572868
  297.5 22.1 %copy-start.86 = (f32[128,1,1024]{2,0,1:T(8,128)S(1)}, f32[128,1,1024]{2,0,1:T(8,128)}, u32[]{:S(2)}) copy-start(f32[128,1,1024]{2,0,1:T(8,128)} %get-tuple-element.465) | copy-start | bytes 1572868
  297.5 23.5 %copy-start.85 = (f32[128,1,1024]{2,0,1:T(8,128)S(1)}, f32[128,1,1024]{2,0,1:T(8,128)}, u32[]{:S(2)}) copy-start(f32[128,1,1024]{2,0,1:T(8,128)} %get-tuple-element.466) | copy-start | bytes 1572868
  297.5 24.8 %copy-start.84 = (f32[128,1,1024]{2,0,1:T(8,128)S(1)}, f32[128,1,1024]{2,0,1:T(8,128)}, u32[]{:S(2)}) copy-start(f32[128,1,1024]{2,0,1:T(8,128)} %get-tuple-element.467) | copy-start | bytes 1572868
  297.5 26.1 %copy-start.81 = (f32[128,1,1024]{2,0,1:T(8,128)S(1)}, f32[128,1,1024]{2,0,1:T(8,128)}, u32[]{:S(2)}) copy-start(f32[128,1,1024]{2,0,1:T(8,128)} %get-tuple-element.362) | copy-start | bytes 1572868
  297.5 27.5 %copy-start.80 = (f32[128,1,1024]{2,0,1:T(8,128)S(1)}, f32[128,1,1024]{2,0,1:T(8,128)}, u32[]{:S(2)}) copy-start(f32[128,1,1024]{2,0,1:T(8,128)} %get-tuple-element.363) | copy-start | bytes 1572868
  298.9 27.4 %copy-start.76 = (f32[128,1,1024]{2,0,1:T(8,128)S(1)}, f32[128,1,1024]{2,0,1:T(8,128)}, u32[]{:S(2)}) copy-start(f32[128,1,1024]{2,0,1:T(8,128)} %get-tuple-element.351) | copy-start | bytes 1572868
  299.8 27.8 %copy-start.75 = (f32[128,1,1024]{2,0,1:T(8,128)S(1)}, f32[128,1,1024]{2,0,1:T(8,128)}, u32[]{:S(2)}) copy-start(f32[128,1,1024]{2,0,1:T(8,128)} %get-tuple-element.352) | copy-start | bytes 1572868
  427.4 44.5 %copy-start.64 = (f32[2048,512]{1,0:T(8,128)}, f32[2048,512]{1,0:T(8,128)S(1)}, u32[]{:S(2)}) copy-start(f32[2048,512]{1,0:T(8,128)S(1)} %get-tuple-element.536) | copy-start | bytes 12582916
  494.4 22.3 %slice-start = ((s8[8388608]{0:T(1024)(128)(4,1)}), s8[4194304]{0:T(1024)(128)(4,1)S(1)}, s32[]{:S(2)}) async-start(s8[8388608]{0:T(1024)(128)(4,1)} %bitcast.251), calls=%async_computation.1 | async-start | bytes 8388608
  526.1 35.4 %copy-start.8 = (f32[128,1,1024]{2,1,0:T(1,128)S(1)}, f32[128,1,1024]{2,1,0:T(1,128)}, u32[]{:S(2)}) copy-start(f32[128,1,1024]{2,1,0:T(1,128)} %copy-done.7) | copy-start | bytes 1572868
  526.1 35.4 %copy-start.11 = (f32[128,1,1024]{2,1,0:T(1,128)S(1)}, f32[128,1,1024]{2,1,0:T(1,128)}, u32[]{:S(2)}) copy-start(f32[128,1,1024]{2,1,0:T(1,128)} %copy-done.10) | copy-start | bytes 1572868
  526.1 35.4 %copy-start.14 = (f32[128,1,1024]{2,1,0:T(1,128)S(1)}, f32[128,1,1024]{2,1,0:T(1,128)}, u32[]{:S(2)}) copy-start(f32[128,1,1024]{2,1,0:T(1,128)} %copy-done.13) | copy-start | bytes 1572868
  616.9 23.4 %copy-start.99 = (f32[15,1024]{1,0:T(8,128)S(1)}, f32[15,1024]{1,0:T(8,128)}, u32[]{:S(2)}) copy-start(f32[15,1024]{1,0:T(8,128)} %slice.950) | copy-start | bytes 184324
  616.9 23.4 %copy-start.100 = (f32[15,1024]{1,0:T(8,128)S(1)}, f32[15,1024]{1,0:T(8,128)}, u32[]{:S(2)}) copy-start(f32[15,1024]{1,0:T(8,128)} %slice.917) | copy-start | bytes 184324
  633.9 28.9 %copy-start.112 = (f32[1,1024]{1,0:T(1,128)S(1)}, f32[1,1024]{1,0:T(1,128)}, u32[]{:S(2)}) copy-start(f32[1,1024]{1,0:T(1,128)} %slice.1112) | copy-start | bytes 12292
  633.9 30.6 %copy-start.113 = (f32[1,1024]{1,0:T(1,128)S(1)}, f32[1,1024]{1,0:T(1,128)}, u32[]{:S(2)}) copy-start(f32[1,1024]{1,0:T(1,128)} %slice.1089) | copy-start | bytes 12292
  727.2 30.0 %copy-start.103 = (f32[1024]{0:T(1024)S(1)}, f32[1024]{0:T(1024)}, u32[]{:S(2)}) copy-start(f32[1024]{0:T(1024)} %custom-call.1) | copy-start | bytes 12292
  776.9 21.3 %copy-start.6 = (f32[2048,1024]{1,0:T(8,128)S(1)}, f32[2048,1024]{1,0:T(8,128)}, u32[]{:S(2)}) copy-start(f32[2048,1024]{1,0:T(8,128)} %get-tuple-element.326) | copy-start | bytes 25165828
  820.0 54.1 %copy-start.108 = (f32[2048]{0:T(1024)S(1)}, f32[2048]{0:T(1024)}, u32[]{:S(2)}) copy-start(f32[2048]{0:T(1024)} %get-tuple-element.519) | copy-start | bytes 24580
  831.8 48.8 %copy-start.127 = (f32[512]{0:T(512)S(1)}, f32[512]{0:T(512)}, u32[]{:S(2)}) copy-start(f32[512]{0:T(512)} %param.31) | copy-start | bytes 6148
  (99 other events, 786.5 us)
Sparse Core Ops, SparseCore 0:
  820.1 281.3 all-reduce.67
where the time goes:
time: 1140 us; the launch traced here: 1120 us
  local copies, waits for them, and re-layouts  423 us (37%)
  other arithmetic  237 us (21%)
  waiting for transfers between devices  210 us (18%)
  matrix products  159 us (14%)
  blocking collectives  75.4 us (7%)
  between operations  16.4 us (1%)
    psum x1, waiting for transfers between devices, per_device(): lax.psum((grad_norm_gain, grad_w_gates, grad_gate_bias, grad_w_out, grad_...  210 us
    slice x94, local copies, waits for them, and re-layouts, block_scan(): lax.associative_scan(combine, (run_decay, run_state), axis=0, reverse=rev...  74.6 us
    slice x2, local copies, waits for them, and re-layouts, block_scan(): step_decay = decay_blocks[:, place]  61.8 us
    slice x2, local copies, waits for them, and re-layouts, block_scan(): step_drive = drive_blocks[:, place]  60.8 us
    dot_general x4, matrix products, times_transposed(): lax.dot_general(left, right, (((1,), (1,)), ((), ())), preferred_element_...  48.2 us
    add x29, other arithmetic, combine(): return (earlier[0] * later[0], later[0] * earlier[1] + later[1])  45.7 us
    dot_general x1, matrix products, per_device(): jnp.dot(normed_two_low, w_up, preferred_element_type=jnp.float32) + up_bias  43.8 us
    unnamed x288, local copies, waits for them, and re-layouts  43.5 us
  transfers between devices with their start and end apart: 1, of which 1 were waited for; matrix products, arithmetic and copies ran while one was open for 2% of the time, Pallas kernels for 0%

commit v1 on v0

v1 whole, which is shorter than its diff:
```python
import functools

import jax
import jax.numpy as jnp
from jax import lax
from jax.experimental import pallas as pl
from jax.experimental.pallas import tpu as pltpu
from jax.sharding import PartitionSpec as P

MESH = pl.DeviceIdType.MESH
F32 = jnp.float32
BF16 = jnp.bfloat16
epsilon = 1e-06
SUB = 8
LANES = 256


def flip(v, w):
    return v + w - 2 * w * ((v // w) % 2)


def dot(a, b):
    return jnp.dot(a, b, preferred_element_type=F32)


def dot_t(a, b):
    return lax.dot_general(a, b, (((1,), (1,)), ((), ())), preferred_element_type=F32)


def fold_rows(v):
    return jnp.sum(v.reshape(v.shape[0] // SUB, SUB, v.shape[1]), axis=0)


def inv_rms(v):
    return lax.rsqrt(jnp.mean(v * v, axis=-1, keepdims=True) + epsilon)


def to_steps(block, scratch):
    pieces, steps, n = block.shape
    flat = block.astype(F32).reshape(pieces * steps, n)
    parts = []
    for k in range(n // 128):
        scratch[k] = flat[:, k * 128 : (k + 1) * 128]
        parts.append(
            jnp.concatenate([scratch[k, pl.ds(r, pieces, stride=steps), :] for r in range(steps)], axis=0)
        )
    return jnp.concatenate(parts, axis=1)


def from_steps(value, scratch, steps):
    n = value.shape[1]
    parts = []
    for k in range(n // 128):
        for r in range(steps):
            scratch[k, pl.ds(r, SUB, stride=steps), :] = value[
                r * SUB : (r + 1) * SUB, k * 128 : (k + 1) * 128
            ]
        parts.append(scratch[k])
    return jnp.concatenate(parts, axis=1).reshape(SUB, steps, n)


def gates_kernel(
    piece, short_ref, long_ref, x_ref, gain_ref, wg_ref, bias_ref,
    a_ref, b_ref, zc_ref, fc_ref, ic_ref, xp_ref, nt_ref, prod_ref, sum_ref, perm,
):
    i = pl.program_id(0)
    steps = x_ref.shape[1]
    rows = steps * SUB
    hid = wg_ref.shape[1] // 3
    source = to_steps(x_ref[...], perm)
    xp_ref[...] = source.astype(BF16)
    normed = (source * inv_rms(source) * gain_ref[...]).astype(BF16)
    nt_ref[...] = normed.T

    group = lax.axis_index("batch")
    half = short_ref.shape[0]
    first = lax.axis_index("seq") * piece * SUB
    row = lax.broadcasted_iota(jnp.int32, (rows, 128), 0)
    pos = first + (row % SUB) * piece + i * steps + row // SUB
    short = group < half
    srow = jnp.minimum(group, half - 1)
    lrow = jnp.maximum(group - half, 0)
    begins = jnp.zeros((rows, 128), jnp.bool_)
    at = jnp.int32(0)
    for k in range(short_ref.shape[1]):
        begins = begins | (pos == jnp.where(short, at, -1))
        at = at + short_ref[srow, k]
    at = jnp.int32(0)
    for k in range(long_ref.shape[1]):
        begins = begins | (pos == jnp.where(short, -1, at))
        at = at + long_ref[lrow, k]
    keep = jnp.where(begins, 0.0, 1.0).astype(F32)

    @pl.when(i == 0)
    def _():
        prod_ref[...] = jnp.ones_like(prod_ref)
        sum_ref[...] = jnp.zeros_like(sum_ref)

    for j in range(hid // LANES):
        cols = [slice(g * hid + j * LANES, g * hid + (j + 1) * LANES) for g in range(3)]
        zf, zi, zc = [dot(normed, wg_ref[:, c]) + bias_ref[:, c] for c in cols]
        f = 1.0 / (1.0 + jnp.exp(-zf))
        g = 1.0 / (1.0 + jnp.exp(-zi))
        inv = 1.0 / (f + g)
        a = f * inv * jnp.concatenate([keep] * (LANES // 128), axis=1)
        b = g * inv
        here = cols[0]
        a_ref[:, here] = a
        b_ref[:, here] = b
        zc_ref[:, here] = zc
        fc_ref[:, here] = (1.0 - f).astype(BF16)
        ic_ref[:, here] = (1.0 - g).astype(BF16)
        u = b * zc
        prod = prod_ref[:, here]
        total = sum_ref[:, here]
        for r in range(steps):
            sl = slice(r * SUB, (r + 1) * SUB)
            prod = prod * a[sl]
            total = total * a[sl] + u[sl]
        prod_ref[:, here] = prod
        sum_ref[:, here] = total


def carry_kernel(devices, reverse, prod_ref, sum_ref, out_ref, mine, got, ssem, rsem):
    s = lax.axis_index("seq")
    b = lax.axis_index("batch")
    bar = pltpu.get_barrier_semaphore()
    others = [lax.rem(s + k, devices) for k in range(1, devices)]
    for o in others:
        pl.semaphore_signal(bar, inc=1, device_id=(o, b), device_id_type=MESH)
    order = list(range(SUB))[::-1] if reverse else list(range(SUB))
    width = prod_ref.shape[1]
    prod = jnp.ones((1, width), F32)
    total = jnp.zeros((1, width), F32)
    for c in order:
        prod = prod * prod_ref[c : c + 1, :]
        total = total * prod_ref[c : c + 1, :] + sum_ref[c : c + 1, :]
    mine[0:1, :] = prod
    mine[1:2, :] = total
    pl.semaphore_wait(bar, devices - 1)
    copies = []
    for k in range(1, devices):
        copies.append(
            pltpu.make_async_remote_copy(
                src_ref=mine, dst_ref=got.at[k - 1], send_sem=ssem.at[k - 1], recv_sem=rsem.at[k - 1],
                device_id=(others[k - 1], b), device_id_type=MESH,
            )
        )
        copies[-1].start()
    for c in copies:
        c.wait()
    state = jnp.zeros((1, width), F32)
    for turn in range(devices - 1):
        if reverse:
            owner = devices - 1 - turn
            ahead = owner > s
            back = lax.rem(s - owner + devices, devices)
        else:
            owner = turn
            ahead = owner < s
            back = lax.rem(s - owner + devices, devices)
        slot = jnp.where(back == 0, 0, back - 1)
        new = got[slot, 0:1, :] * state + got[slot, 1:2, :]
        state = jnp.where(ahead, new, state)
    for c in order:
        out_ref[c : c + 1, :] = state
        state = prod_ref[c : c + 1, :] * state + sum_ref[c : c + 1, :]


def carry(devices, reverse, prod, total):
    width = prod.shape[1]
    return pl.pallas_call(
        functools.partial(carry_kernel, devices, reverse),
        out_shape=jax.ShapeDtypeStruct((SUB, width), F32),
        in_specs=[pl.BlockSpec(memory_space=pltpu.VMEM)] * 2,
        out_specs=pl.BlockSpec(memory_space=pltpu.VMEM),
        scratch_shapes=[
            pltpu.VMEM((SUB, width), F32),
            pltpu.VMEM((devices - 1, SUB, width), F32),
            pltpu.SemaphoreType.DMA((devices - 1,)),
            pltpu.SemaphoreType.DMA((devices - 1,)),
        ],
        compiler_params=pltpu.CompilerParams(
            collective_id=1 + int(reverse), has_side_effects=True
        ),
    )(prod, total)


KA = 0.3275911 * 2.0**-0.5
ERF = [0.5 * c for c in (0.254829592, -0.284496736, 1.421413741, -1.453152027, 1.061405429)]
PHI = 0.3989422804014327


def gelu_parts(x):
    t = 1.0 / (1.0 + KA * jnp.abs(x))
    e = jnp.exp2(x * x * (-0.5 * 1.4426950408889634))
    poly = t * (ERF[0] + t * (ERF[1] + t * (ERF[2] + t * (ERF[3] + t * ERF[4]))))
    tail = poly * e
    phi = jnp.where(x >= 0.0, 1.0 - tail, tail)
    return x * phi, phi + x * (e * PHI)


def mlp_kernel(
    a_ref, b_ref, zc_ref, xp_ref, dy_ref, carry_ref, wo_ref, wu_ref, wd_ref,
    obias_ref, gain_ref, ubias_ref, dbias_ref,
    s_ref, sb_ref, act_ref, gu_ref, dyt_ref, n2t_ref, grt_ref, gres_ref, gs_ref, result_ref,
    mu_ref, gdb_ref, gub_ref, ggain_ref, gob_ref,
    state, prod, perm,
):
    i = pl.program_id(0)
    steps = dy_ref.shape[1]

    @pl.when(i == 0)
    def _():
        state[...] = carry_ref[...]
        prod[...] = jnp.ones_like(prod)
        for ref in (mu_ref, gdb_ref, gub_ref, ggain_ref, gob_ref):
            ref[...] = jnp.zeros_like(ref)

    st = state[...]
    for r in range(steps):
        sl = slice(r * SUB, (r + 1) * SUB)
        st = a_ref[sl, :] * st + b_ref[sl, :] * zc_ref[sl, :]
        s_ref[sl, :] = st
    state[...] = st
    sb = s_ref[...].astype(BF16)
    sb_ref[...] = sb
    source = xp_ref[...].astype(F32)
    resid = source + dot(sb, wo_ref[...]) + obias_ref[...]
    scale = inv_rms(resid)
    n2 = (resid * scale * gain_ref[...]).astype(BF16)
    n2t_ref[...] = n2.T
    dy32 = to_steps(dy_ref[...], perm)
    dy = dy32.astype(BF16)
    dyt_ref[...] = dy.T
    gdb_ref[...] += fold_rows(dy32)
    down = None
    gn2 = None
    for j in range(wu_ref.shape[1] // LANES):
        cols = slice(j * LANES, (j + 1) * LANES)
        upper = dot(n2, wu_ref[:, cols]) + ubias_ref[:, cols]
        act, slope = gelu_parts(upper)
        act = act.astype(BF16)
        act_ref[:, cols] = act
        gact = dot_t(dy, wd_ref[cols, :])
        gu = (gact * slope).astype(BF16)
        gu_ref[:, cols] = gu
        gub_ref[:, cols] += fold_rows(gu.astype(F32))
        d = dot(act, wd_ref[cols, :])
        n = dot_t(gu, wu_ref[:, cols])
        down = d if down is None else down + d
        gn2 = n if gn2 is None else gn2 + n
    result = resid + down + dbias_ref[...]
    result_ref[...] = from_steps(result, perm, steps).astype(BF16)
    w = gn2 * gain_ref[...]
    ggain_ref[...] += fold_rows(gn2 * resid * scale)
    gres = dy32 + scale * w - resid * (scale * scale * scale) * jnp.mean(
        w * resid, axis=-1, keepdims=True
    )
    gres_ref[...] = gres
    gr = gres.astype(BF16)
    gob_ref[...] += fold_rows(gr.astype(F32))
    grt_ref[...] = gr.T
    gs = dot_t(gr, wo_ref[...])
    gs_ref[...] = gs
    pr = prod[...]
    mu = mu_ref[...]
    for r in range(steps):
        sl = slice(r * SUB, (r + 1) * SUB)
        pr = pr * a_ref[sl, :]
        mu = mu + pr * gs[sl, :]
    prod[...] = pr
    mu_ref[...] = mu


def back_kernel(
    a_ref, b_ref, zc_ref, fc_ref, ic_ref, s_ref, gs_ref, xp_ref, gres_ref, carry_ref, wg_ref,
    gain_ref,
    gm_ref, gin_ref, ggb_ref, ggain_ref,
    state, perm,
):
    i = pl.program_id(0)
    steps = gin_ref.shape[1]
    hid = wg_ref.shape[1] // 3

    @pl.when(i == 0)
    def _():
        state[...] = carry_ref[...]
        for ref in (ggb_ref, ggain_ref):
            ref[...] = jnp.zeros_like(ref)

    gn = None
    for j in range(hid // LANES):
        here = slice(j * LANES, (j + 1) * LANES)
        mu = state[:, here]
        lams = [None] * steps
        for r in range(steps - 1, -1, -1):
            sl = slice(r * SUB, (r + 1) * SUB)
            lams[r] = gs_ref[sl, here] + mu
            mu = a_ref[sl, here] * lams[r]
        state[:, here] = mu
        lam = jnp.concatenate(lams, axis=0)
        gzc = lam * b_ref[:, here]
        big = gzc * (s_ref[:, here] - zc_ref[:, here])
        parts = (
            (big * fc_ref[:, here].astype(F32)).astype(BF16),
            (-big * ic_ref[:, here].astype(F32)).astype(BF16),
            gzc.astype(BF16),
        )
        for g in range(3):
            cols = slice(g * hid + j * LANES, g * hid + (j + 1) * LANES)
            gm_ref[:, cols] = parts[g]
            ggb_ref[:, cols] += fold_rows(parts[g].astype(F32))
            n = dot_t(parts[g], wg_ref[:, cols])
            gn = n if gn is None else gn + n
    source = xp_ref[...].astype(F32)
    scale = inv_rms(source)
    w = gn * gain_ref[...]
    ggain_ref[...] += fold_rows(gn * source * scale)
    gin = gres_ref[...] + scale * w - source * (scale * scale * scale) * jnp.mean(
        w * source, axis=-1, keepdims=True
    )
    gin_ref[...] = from_steps(gin, perm, steps)


def bits_of(size):
    w = 1
    out = []
    while w < size:
        out.append(w); w *= 2
    return out

class Plan:
    def __init__(self, seq, batch, rows):
        sb = [("seq", w) for w in bits_of(seq)]
        bb = [("batch", w) for w in bits_of(batch)][1:]
        self.orders = [sb + bb, sb[::-1] + bb, bb[:1] + sb + bb[1:], sb + bb, sb[::-1] + bb, bb[:1] + sb[::-1] + bb[1:]]
        self.K = len(sb) + len(bb)
        self.rows = rows
        self.sizes = [rows]
        self.halve = []
        for k in range(self.K + 1):
            h = self.sizes[-1] >= 16
            self.halve.append(h)
            self.sizes.append(self.sizes[-1] // 2 if h else self.sizes[-1])
        self.stages = 2 * (self.K + 1)
        self.colors = len(self.orders)
        self.base = []
        tot = 0
        for k in range(self.K + 1):
            self.base.append(tot); tot += self.sizes[k + 1]
        self.recv_rows = tot

def pick(color, values):
    out = values[-1]
    for i in range(len(values) - 1):
        out = jnp.where(color == i, values[i], out)
    return out

def step_info(plan, k, color):
    s = lax.axis_index("seq"); b = lax.axis_index("batch")
    if k == 0:
        return b % 2, (s, flip(b, 1))
    mine, ps, pb = [], [], []
    for order in plan.orders:
        axis, w = order[k - 1]
        if axis == "seq":
            mine.append((s // w) % 2); ps.append(flip(s, w)); pb.append(b)
        else:
            mine.append((b // w) % 2); ps.append(s); pb.append(flip(b, w))
    return pick(color, mine), (pick(color, ps), pick(color, pb))

def offsets(plan, c, color, upto):
    off = c * plan.rows
    for k in range(upto):
        if plan.halve[k]:
            bit, _ = step_info(plan, k, color)
            off = off + bit * plan.sizes[k + 1]
    return pl.multiple_of(off, 8)

def copy_of(plan, acc, recv, ssem, rsem, c, j):
    color = c % plan.colors
    slot = color * 2 + (c // plan.colors) % 2
    K = plan.K
    if j <= K:
        k = j
        bit, dev = step_info(plan, k, color)
        n = plan.sizes[k + 1]
        base = offsets(plan, c, color, k)
        src = base + (1 - bit) * n if plan.halve[k] else base
        return pltpu.make_async_remote_copy(
            src_ref=acc.at[pl.ds(pl.multiple_of(src, 8), n)], dst_ref=recv.at[slot, pl.ds(plan.base[k], n)],
            send_sem=ssem.at[slot, j], recv_sem=rsem.at[slot, j], device_id=dev, device_id_type=MESH)
    k = 2 * K + 1 - j
    if not plan.halve[k]:
        return None
    bit, dev = step_info(plan, k, color)
    n = plan.sizes[k + 1]
    mine = offsets(plan, c, color, k + 1)
    return pltpu.make_async_remote_copy(
        src_ref=acc.at[pl.ds(mine, n)], dst_ref=acc.at[pl.ds(mine, n)],
        send_sem=ssem.at[slot, j], recv_sem=rsem.at[slot, j], device_id=dev, device_id_type=MESH)

def finish(plan, acc, recv, ssem, rsem, free, c, j):
    cp = copy_of(plan, acc, recv, ssem, rsem, c, j)
    if cp is None:
        return
    cp.wait()
    if j <= plan.K:
        color = c % plan.colors
        slot = color * 2 + (c // plan.colors) % 2
        n = plan.sizes[j + 1]
        if plan.halve[j]:
            _, dev = step_info(plan, j, color)
            pl.semaphore_signal(free.at[slot, j], inc=1, device_id=dev, device_id_type=MESH)
        off = offsets(plan, c, color, j + 1)
        acc[pl.ds(off, n), :] = acc[pl.ds(off, n), :] + recv[slot, pl.ds(plan.base[j], n), :]

def tick(plan, nchunks, acc, recv, ssem, rsem, free, t, done, L=1):
    for j in range(plan.stages, -1, -1):
        c = t - L * j
        @pl.when((c >= 0) & (c < nchunks))
        def _():
            if j > 0:
                finish(plan, acc, recv, ssem, rsem, free, c, j - 1)
            if j < plan.stages:
                cp = copy_of(plan, acc, recv, ssem, rsem, c, j)
                if cp is not None:
                    if j > plan.K:
                        color = c % plan.colors
                        slot = color * 2 + (c // plan.colors) % 2
                        pl.semaphore_wait(free.at[slot, 2 * plan.K + 1 - j], 1)
                    cp.start()
            else:
                done(c)

def greet(plan, extra=()):
    s = lax.axis_index("seq"); b = lax.axis_index("batch")
    who = [(s, flip(b, 1))]
    for axis, w in plan.orders[0]:
        who.append((flip(s, w), b) if axis == "seq" else (s, flip(b, w)))
    who += list(extra)
    bar = pltpu.get_barrier_semaphore()
    for p in who:
        pl.semaphore_signal(bar, inc=1, device_id=p, device_id_type=MESH)
    pl.semaphore_wait(bar, len(who))


def small_copy(plan, small, got, ssem, rsem, k):
    _, dev = step_info(plan, k, 0)
    return pltpu.make_async_remote_copy(
        src_ref=small, dst_ref=got.at[k], send_sem=ssem.at[k], recv_sem=rsem.at[k],
        device_id=dev, device_id_type=MESH)


def ar_kernel(plan, nchunks, lag, x_hbm, small_in, o_hbm, small_out,
              acc, recv, ssem, rsem, free, isem, osem, small, got, s2sem, r2sem):
    cp = pltpu.make_async_copy(x_hbm, acc, isem)
    cp.start()
    small[...] = small_in[...]
    greet(plan)
    cp.wait()
    def out_copy(c):
        rows = pl.ds(pl.multiple_of(c * plan.rows, 8), plan.rows)
        return pltpu.make_async_copy(acc.at[rows], o_hbm.at[rows], osem.at[c])
    def body(t, _):
        for k in range(plan.K + 2):
            @pl.when(t == k * lag)
            def _():
                if k > 0:
                    small_copy(plan, small, got, s2sem, r2sem, k - 1).wait()
                    small[...] = small[...] + got[k - 1]
                if k <= plan.K:
                    small_copy(plan, small, got, s2sem, r2sem, k).start()
        tick(plan, nchunks, acc, recv, ssem, rsem, free, t, lambda c: out_copy(c).start(), lag)
        return 0
    lax.fori_loop(0, nchunks + lag * plan.stages, body, 0)
    small_out[...] = small[...]
    def wait(c, _):
        out_copy(c).wait()
        return 0
    lax.fori_loop(0, nchunks, wait, 0)

def all_reduce(x, small, seq, batch, chunk_rows, lag):
    plan = Plan(seq, batch, chunk_rows)
    n = x.shape[0] // chunk_rows
    slots = plan.colors * 2
    any_space = pl.BlockSpec(memory_space=pl.ANY)
    vmem = pl.BlockSpec(memory_space=pltpu.VMEM)
    return pl.pallas_call(
        functools.partial(ar_kernel, plan, n, lag),
        out_shape=[jax.ShapeDtypeStruct(x.shape, F32), jax.ShapeDtypeStruct(small.shape, F32)],
        in_specs=[any_space, vmem],
        out_specs=[any_space, vmem],
        scratch_shapes=[
            pltpu.VMEM(x.shape, F32),
            pltpu.VMEM((slots, plan.recv_rows, x.shape[1]), F32),
            pltpu.SemaphoreType.DMA((slots, plan.stages)),
            pltpu.SemaphoreType.DMA((slots, plan.stages)),
            pltpu.SemaphoreType.REGULAR((slots, plan.K + 1)),
            pltpu.SemaphoreType.DMA,
            pltpu.SemaphoreType.DMA((n,)),
            pltpu.VMEM(small.shape, F32),
            pltpu.VMEM((plan.K + 1,) + small.shape, F32),
            pltpu.SemaphoreType.DMA((plan.K + 1,)),
            pltpu.SemaphoreType.DMA((plan.K + 1,)),
        ],
        compiler_params=pltpu.CompilerParams(collective_id=0, has_side_effects=True, vmem_limit_bytes=60 << 20),
    )(x, small)


def full(shape):
    return pl.BlockSpec(shape, lambda i: (0,) * len(shape), pipeline_mode=pl.Buffered(1))


def held(shape):
    return pl.BlockSpec(shape, lambda i: (0,) * len(shape))


def local_part(mesh_seq, inputs, cotangent, short_lengths, long_lengths, norm_gain, w_gates, gate_bias, w_out,
               out_bias, mlp_gain, w_up, up_bias, w_down, down_bias, tile=256):
    tok, d = inputs.shape[1:]
    hid = w_out.shape[0]
    ff = w_up.shape[1]
    piece = tok // SUB
    steps = tile // SUB
    grid = tok // tile
    x = inputs.reshape(SUB, piece, d)
    dy = cotangent.reshape(SUB, piece, d)
    gain1 = norm_gain.reshape(1, d)
    gain2 = mlp_gain.reshape(1, d)
    sds = jax.ShapeDtypeStruct
    rows = lambda n: pl.BlockSpec((tile, n), lambda i: (i, 0))
    natural = pl.BlockSpec((SUB, steps, d), lambda i: (0, i, 0))
    turned = pl.BlockSpec((d, tile), lambda i: (0, i))
    params = pltpu.CompilerParams(
        dimension_semantics=("arbitrary",), vmem_limit_bytes=56 << 20
    )
    a, b, zc, fc, ic, xp, nt, prod, total = pl.pallas_call(
        functools.partial(gates_kernel, piece),
        grid=(grid,),
        in_specs=[
            pl.BlockSpec(memory_space=pltpu.SMEM), pl.BlockSpec(memory_space=pltpu.SMEM),
            natural, full((1, d)), full((d, 3 * hid)), full((1, 3 * hid)),
        ],
        out_specs=[rows(hid)] * 5 + [rows(d), turned, held((SUB, hid)), held((SUB, hid))],
        out_shape=[sds((tok, hid), F32)] * 3 + [sds((tok, hid), BF16)] * 2
        + [sds((tok, d), BF16), sds((d, tok), BF16), sds((SUB, hid), F32), sds((SUB, hid), F32)],
        scratch_shapes=[pltpu.VMEM((d // 128, tile, 128), F32)],
        compiler_params=params,
    )(short_lengths, long_lengths, x, gain1, w_gates, gate_bias.reshape(1, 3 * hid))

    enter = carry(mesh_seq, False, prod, total)

    outs = pl.pallas_call(
        mlp_kernel,
        grid=(grid,),
        in_specs=[rows(hid)] * 3 + [rows(d), natural, full((SUB, hid)), full((hid, d)), full((d, ff)), full((ff, d)),
                  full((1, d)), full((1, d)), full((1, ff)), full((1, d))],
        out_specs=[rows(hid), rows(hid), rows(ff), rows(ff), turned, turned, turned, rows(d), rows(hid), natural,
                   held((SUB, hid)), held((SUB, d)), held((SUB, ff)), held((SUB, d)), held((SUB, d))],
        out_shape=[sds((tok, hid), F32), sds((tok, hid), BF16), sds((tok, ff), BF16), sds((tok, ff), BF16),
                   sds((d, tok), BF16), sds((d, tok), BF16), sds((d, tok), BF16), sds((tok, d), F32),
                   sds((tok, hid), F32), sds((SUB, piece, d), BF16),
                   sds((SUB, hid), F32), sds((SUB, d), F32), sds((SUB, ff), F32), sds((SUB, d), F32), sds((SUB, d), F32)],
        scratch_shapes=[pltpu.VMEM((SUB, hid), F32), pltpu.VMEM((SUB, hid), F32), pltpu.VMEM((d // 128, tile, 128), F32)],
        compiler_params=params,
    )(a, b, zc, xp, dy, enter, w_out, w_up, w_down, out_bias.reshape(1, d), gain2, up_bias.reshape(1, ff),
      down_bias.reshape(1, d))
    s, sb, act, gu, dyt, n2t, grt, gres, gs, result, mu, gdb, gub, ggain2, gob = outs

    enter_back = carry(mesh_seq, True, prod, mu)

    back = lambda n: pl.BlockSpec((tile, n), lambda i: (grid - 1 - i, 0))
    gm, gin, ggb, ggain1 = pl.pallas_call(
        back_kernel,
        grid=(grid,),
        in_specs=[back(hid)] * 7 + [back(d), back(d), full((SUB, hid)), full((d, 3 * hid)), full((1, d))],
        out_specs=[back(3 * hid), pl.BlockSpec((SUB, steps, d), lambda i: (0, grid - 1 - i, 0)),
                   held((SUB, 3 * hid)), held((SUB, d))],
        out_shape=[sds((tok, 3 * hid), BF16), sds((SUB, piece, d), F32), sds((SUB, 3 * hid), F32), sds((SUB, d), F32)],
        scratch_shapes=[pltpu.VMEM((SUB, hid), F32), pltpu.VMEM((d // 128, tile, 128), F32)],
        compiler_params=params,
    )(a, b, zc, fc, ic, s, gs, xp, gres, enter_back, w_gates, gain1)
    return (result, gin, (nt, gm), (grt, sb), (n2t, gu), (dyt, act),
            (ggain1, ggb, gob, ggain2, gub, gdb))


def blocks_of(v):
    d, n = v.shape
    return v.reshape(d, n // LANES, LANES).transpose(1, 0, 2).reshape(-1, LANES)


def unblock(v, d):
    n = v.shape[0] // d
    return v.reshape(n, d, LANES).transpose(1, 0, 2).reshape(d, n * LANES)


def per_device(seq, batch, *args):
    result, gin, gates, out, up, down, small = local_part(seq, *args)
    inputs = args[0]
    d = inputs.shape[2]
    big = [dot(*pair) for pair in (down, up, out, gates)]
    vecs = [jnp.sum(v, axis=0) for v in small]
    flat = jnp.concatenate(vecs)
    lines = -(-flat.shape[0] // (8 * LANES)) * 8
    flat = jnp.pad(flat, (0, lines * LANES - flat.shape[0])).reshape(lines, LANES)
    total, flat = all_reduce(jnp.concatenate([blocks_of(v) for v in big]), flat, seq, batch, d, 3)
    flat = flat.reshape(-1)
    grads = []
    at = 0
    for v in big:
        n = v.shape[1] // LANES * d
        grads.append(unblock(total[at : at + n], d))
        at += n
    svecs = []
    at = 0
    for v in vecs:
        svecs.append(flat[at : at + v.shape[0]])
        at += v.shape[0]
    g_down, g_up, g_out, g_gates = grads
    ggain1, ggb, gob, ggain2, gub, gdb = svecs
    return (result.reshape(inputs.shape), gin.reshape(inputs.shape), ggain1, g_gates, ggb, g_out.T, gob,
            ggain2, g_up, gub, g_down.T, gdb)


def solution(mesh):
    rows = P("batch", "seq", None)
    return jax.shard_map(
        functools.partial(per_device, mesh.shape["seq"], mesh.shape["batch"]),
        mesh=mesh,
        in_specs=(rows, rows) + (P(),) * 12,
        out_specs=(rows, rows) + (P(),) * 10,
        check_vma=False,
    )
```

time: 1140 us -> 361 us (0.32); the launches traced: 1120 us -> 360 us
  local copies, waits for them, and re-layouts: 423 us -> 62.9 us
  Pallas kernels: 0 us -> 257 us
  other arithmetic: 237 us -> 16 us
  waiting for transfers between devices: 210 us -> 0 us
  matrix products: 159 us -> 22.8 us
  blocking collectives: 75.4 us -> 0 us
  between operations: 16.4 us -> 0.92 us
    pallas_call x0 -> x6, Pallas kernels: none -> 257 us  [the longest x1 140 us: all_reduce(): pl.pallas_call(functools.partial(ar_kernel, plan, n, lag), out_shape=[jax...]
    psum x1 -> x0, waiting for transfers between devices: 210 us -> none  [per_device(): lax.psum((grad_norm_gain, grad_w_gates, grad_gate_bias, grad_w_out, grad_...]
    slice x105 -> x5, local copies, waits for them, and re-layouts: 222 us -> 15.5 us  [the longest x3 14.9 us: per_device(): grads.append(unblock(total[at:at + n], d))]
    dot_general x12 -> x4, matrix products: 159 us -> 22.8 us  [dot(): return jnp.dot(a, b, preferred_element_type=F32)]
    add x60 -> x0, other arithmetic: 101 us -> none  [the longest x29 45.7 us: combine(): return (earlier[0] * later[0], later[0] * earlier[1] + later[1])]
    mul x7 -> x0, other arithmetic: 80.9 us -> none  [the longest x3 43 us: gate_terms(): return (forget / totals * keep_mask, inputs_gate / totals * candidate)]
    another operation x4 -> x0, local copies, waits for them, and re-layouts: 49.2 us -> none  [the longest x2 25 us: block_scan(): cum_local = jnp.stack(cum_list, axis=1)]
    psum x1 -> x0, blocking collectives: 42.3 us -> none  [per_device(): lax.psum((grad_norm_gain, grad_w_gates, grad_gate_bias, grad_w_out, grad_...]
  transfers between devices with their start and end apart: 1 -> 0, of which waited for: 1 -> 0; matrix products, arithmetic and copies ran while one was open for 2% -> 0% of each run, Pallas kernels for 0% -> 0%
where the time goes in v1:
time: 361 us; the launch traced here: 360 us
  Pallas kernels  257 us (71%)
  local copies, waits for them, and re-layouts  62.9 us (17%)
  matrix products  22.8 us (6%)
  other arithmetic  16 us (4%)
    pallas_call x1, Pallas kernels, all_reduce(): pl.pallas_call(functools.partial(ar_kernel, plan, n, lag), out_shape=[jax...  140 us
    pallas_call x1, Pallas kernels, local_part(): pl.pallas_call(mlp_kernel, grid=(grid,), in_specs=[rows(hid)] * 3 + [rows...  53.8 us
    pallas_call x1, Pallas kernels, local_part(): pl.pallas_call(back_kernel, grid=(grid,), in_specs=[back(hid)] * 7 + [bac...  27.6 us
    dot_general x4, matrix products, dot(): return jnp.dot(a, b, preferred_element_type=F32)  22.8 us
    pallas_call x1, Pallas kernels, local_part(): pl.pallas_call(functools.partial(gates_kernel, piece), grid=(grid,), in_s...  20.4 us
    unnamed x42, local copies, waits for them, and re-layouts  16.3 us
    slice x3, local copies, waits for them, and re-layouts, per_device(): grads.append(unblock(total[at:at + n], d))  14.9 us
    pallas_call x2, Pallas kernels, carry(): pl.pallas_call(functools.partial(carry_kernel, devices, reverse), out_sha...  14.8 us

profile of v1, /device:TPU:0, one launch (start us, length us, event | category | flops | bytes accessed | tf_op | source)
XLA Modules:
  0.0 359.8 jit_solution(9648464662548711636)
XLA Ops:
  0.6 1.3 copy.35.long_ref
  2.0 20.4 %shard_map.229 = (f32[2048,1024]{1,0:T(8,128)}, f32[2048,1024]{1,0:T(8,128)}, f32[2048,1024]{1,0:T(8,128)}, bf16[2048,1024]{1,0:T(8,128)(2,1)}, bf16[2048,1024]{...) custom-call(s32[4,4]{1,0:T(4,128)} %short_ref.1, ...), custom_call_target="tpu_custom_call" | custom-call | tf_op jit(solution)/shard_map/pallas_call | solution.py:539
  22.4 8.2 %shard_map.230.carry_ref = f32[8,1024]{1,0:T(8,128)} custom-call(f32[8,1024]{1,0:T(8,128)} %get-tuple-element.46.prod_ref, f32[8,1024]{1,0:T(8,128)} %get-tuple-element.47.sum_ref), custom_call_target="tpu_custom_call" | custom-call | tf_op jit(solution)/shard_map/pallas_call | solution.py:172
  30.6 53.8 %shard_map.231 = (f32[2048,1024]{1,0:T(8,128)}, bf16[2048,1024]{1,0:T(8,128)(2,1)}, bf16[2048,2048]{1,0:T(8,128)(2,1)}, bf16[2048,2048]{1,0:T(8,128)(2,1)}, bf16...) custom-call(f32[2048,1024]{1,0:T(8,128)} %get-tuple-element.42.a_ref, ...), custom_call_target="tpu_custom_call" | custom-call | tf_op jit(solution)/shard_map/pallas_call | solution.py:555
  84.4 6.6 %shard_map.232.carry_ref = f32[8,1024]{1,0:T(8,128)} custom-call(f32[8,1024]{1,0:T(8,128)} %get-tuple-element.46.prod_ref, f32[8,1024]{1,0:T(8,128)} %get-tuple-element.54.sum_ref), custom_call_target="tpu_custom_call" | custom-call | tf_op jit(solution)/shard_map/pallas_call | solution.py:172
  91.1 27.6 %shard_map.233 = (bf16[2048,3072]{1,0:T(8,128)(2,1)}, f32[8,256,512]{2,1,0:T(8,128)}, f32[8,3072]{1,0:T(8,128)}, f32[8,512]{1,0:T(8,128)}) custom-call(f32[2048,1024]{1,0:T(8,128)} %get-tuple-element.42.a_ref, f32[2048,1024]{1,0:T(8,128)} %get-tuple-element.43.b_ref, f32[2048,1024]{1,0:T(8,128)} %get-tuple-element.44.zc_ref, ...), custom_call_target="tpu_custom_call" | custom-call | tf_op jit(solution)/shard_map/pallas_call | solution.py:575
  118.8 0.7 reduce_sum.54
  119.5 0.9 reduce_sum.55
  120.7 0.6 reshape.130.small_in
  121.3 7.3 %fusion.1 = f32[512,2048]{1,0:T(8,128)S(1)} fusion(bf16[512,2048]{1,0:T(8,128)(2,1)S(1)} %copy-done.10, bf16[2048,2048]{1,0:T(8,128)(2,1)} %get-tuple-element.57), kind=kOutput, calls=%fused_computation.16 | convolution fusion | flops 4294967296 | bytes 14680064 | tf_op jit(solution)/shard_map/dot_general | solution.py:23
  128.6 2.5 copy.60
  131.1 2.3 copy-done.5
  133.5 4.5 %fusion.2 = f32[512,2048]{1,0:T(8,128)S(1)} fusion(bf16[512,2048]{1,0:T(8,128)(2,1)S(1)} %copy-done.9, bf16[2048,2048]{1,0:T(8,128)(2,1)S(1)} %copy-done.5), kind=kOutput, calls=%fused_computation.17 | convolution fusion | flops 4294967296 | bytes 14680064 | tf_op jit(solution)/shard_map/dot_general | solution.py:23
  138.0 2.5 copy.59
  140.5 1.1 copy-done.6
  141.7 2.3 fusion.3
  144.3 1.2 slice-done.2
  145.5 0.6 copy-done.7
  146.2 8.7 %fusion.4 = f32[512,3072]{0,1:T(8,128)} fusion(bf16[512,2048]{1,0:T(8,128)(2,1)S(1)} %copy-done.7, bf16[2048,3072]{1,0:T(8,128)(2,1)S(1)} %bitcast.110), kind=kOutput, calls=%fused_computation.19 | convolution fusion | flops 6442450944 | bytes 20971520 | tf_op jit(solution)/shard_map/dot_general | solution.py:23
  154.9 6.6 %copy.40 = f32[12,512,256]{2,1,0:T(8,128)} copy(f32[12,512,256]{1,2,0:T(8,128)} %bitcast.88) | data formatting | bytes 12582912 | tf_op jit(solution)/shard_map/transpose | solution.py:591
  161.5 14.2 %pad_maximum_fusion.x_hbm = f32[16384,256]{1,0:T(8,128)} fusion(f32[6144,256]{1,0:T(8,128)} %bitcast.79, f32[2048,256]{1,0:T(8,128)S(1)} %bitcast.86, f32[4096,256]{1,0:T(8,128)} %bitcast.85, f32[4096,256]{1,0:T(8,128)} %bitcast.84), kind=kLoop, calls=%fused_computation | loop fusion | flops 12582912 | bytes 33554432 | tf_op jit(solution)/shard_map/concatenate | solution.py:608
  175.7 140.5 %shard_map.234 = (f32[16384,256]{1,0:T(8,128)}, f32[32,256]{1,0:T(8,128)}) custom-call(f32[16384,256]{1,0:T(8,128)} %pad_maximum_fusion.x_hbm, f32[32,256]{1,0:T(8,128)} %reshape.130.small_in), custom_call_target="tpu_custom_call" | custom-call | tf_op jit(solution)/shard_map/pallas_call | solution.py:490
  316.1 5.9 %slice.50 = f32[6144,256]{1,0:T(8,128)} slice(f32[16384,256]{1,0:T(8,128)} %get-tuple-element.71), slice={[10240:16384], [0:256]} | slice | bytes 12582912 | tf_op jit(solution)/shard_map/slice | solution.py:614
  322.0 6.6 %copy.41 = f32[12,512,256]{1,2,0:T(8,128)} copy(f32[12,512,256]{2,1,0:T(8,128)} %bitcast.81) | data formatting | bytes 12582912 | tf_op jit(solution)/shard_map/reshape | solution.py:596
  328.6 6.6 %copy.45 = f32[512,3072]{1,0:T(8,128)} copy(f32[512,3072]{0,1:T(8,128)} %bitcast.80) | data formatting | bytes 12582912
  335.2 7.3 %fusion = (f32[4096,256]{1,0:T(8,128)}, f32[4096,256]{1,0:T(8,128)}) fusion(f32[16384,256]{1,0:T(8,128)} %get-tuple-element.71), kind=kLoop, calls=%fused_computation.15 | loop fusion | bytes 16777216 | tf_op jit(solution)/shard_map/slice | solution.py:614
  342.5 5.3 %copy.44 = f32[512,8,256]{0,2,1:T(8,128)} copy(f32[512,8,256]{2,0,1:T(8,128)} %bitcast.83) | data formatting | bytes 8388608 | tf_op jit(solution)/shard_map/transpose | solution.py:596
  347.8 4.8 %copy.50 = f32[8,64,8,256]{3,2,0,1:T(8,128)} copy(f32[8,64,8,256]{3,2,1,0:T(8,128)} %bitcast.82) | data formatting | bytes 8388608 | tf_op jit(solution)/shard_map/reshape | solution.py:596
  352.7 1.7 slice.53
  354.4 1.8 copy.42
  356.2 0.6 slice.52
  356.8 0.6 copy.54
  (45 shorter events, 2.8 us)
Async XLA Ops:
  91.1 29.4 %copy-start.4 = (f32[8,512]{1,0:T(8,128)S(1)}, f32[8,512]{1,0:T(8,128)}, u32[]{:S(2)}) copy-start(f32[8,512]{1,0:T(8,128)} %get-tuple-element.66) | copy-start | bytes 49156
  91.1 29.4 %copy-start.3 = (f32[8,512]{1,0:T(8,128)S(1)}, f32[8,512]{1,0:T(8,128)}, u32[]{:S(2)}) copy-start(f32[8,512]{1,0:T(8,128)} %get-tuple-element.67) | copy-start | bytes 49156
  91.1 29.5 %copy-start = (f32[8,2048]{1,0:T(8,128)S(1)}, f32[8,2048]{1,0:T(8,128)}, u32[]{:S(2)}) copy-start(f32[8,2048]{1,0:T(8,128)} %get-tuple-element.68) | copy-start | bytes 196612
  91.1 29.5 %copy-start.2 = (f32[8,512]{1,0:T(8,128)S(1)}, f32[8,512]{1,0:T(8,128)}, u32[]{:S(2)}) copy-start(f32[8,512]{1,0:T(8,128)} %get-tuple-element.69) | copy-start | bytes 49156
  91.1 30.2 %copy-start.10 = (bf16[512,2048]{1,0:T(8,128)(2,1)S(1)}, bf16[512,2048]{1,0:T(8,128)(2,1)}, u32[]{:S(2)}) copy-start(bf16[512,2048]{1,0:T(8,128)(2,1)} %get-tuple-element.56) | copy-start | bytes 6291460
  121.3 9.8 %copy-start.9 = (bf16[512,2048]{1,0:T(8,128)(2,1)S(1)}, bf16[512,2048]{1,0:T(8,128)(2,1)}, u32[]{:S(2)}) copy-start(bf16[512,2048]{1,0:T(8,128)(2,1)} %get-tuple-element.58) | copy-start | bytes 6291460
  128.6 4.9 %copy-start.5 = (bf16[2048,2048]{1,0:T(8,128)(2,1)S(1)}, bf16[2048,2048]{1,0:T(8,128)(2,1)}, u32[]{:S(2)}) copy-start(bf16[2048,2048]{1,0:T(8,128)(2,1)} %get-tuple-element.59) | copy-start | bytes 25165828
  133.5 7.1 %copy-start.8 = (bf16[512,2048]{1,0:T(8,128)(2,1)S(1)}, bf16[512,2048]{1,0:T(8,128)(2,1)}, u32[]{:S(2)}) copy-start(bf16[512,2048]{1,0:T(8,128)(2,1)} %get-tuple-element.60) | copy-start | bytes 6291460
  138.0 3.7 %copy-start.6 = (bf16[2048,1024]{1,0:T(8,128)(2,1)S(1)}, bf16[2048,1024]{1,0:T(8,128)(2,1)}, u32[]{:S(2)}) copy-start(bf16[2048,1024]{1,0:T(8,128)(2,1)} %get-tuple-element.61) | copy-start | bytes 12582916
  138.0 6.2 %slice-start = ((s8[12582912]{0:T(1024)(128)(4,1)}), s8[4194304]{0:T(1024)(128)(4,1)S(1)}, s32[]{:S(2)}) async-start(s8[12582912]{0:T(1024)(128)(4,1)} %bitcast.109), calls=%async_computation | async-start | bytes 8388608
  141.7 2.7 slice-start.1
  141.7 3.9 %slice-start.2 = ((s8[12582912]{0:T(1024)(128)(4,1)}), s8[4194304]{0:T(1024)(128)(4,1)S(1)}, s32[]{:S(2)}) async-start(s8[12582912]{0:T(1024)(128)(4,1)} %bitcast.109), calls=%async_computation.2 | async-start | bytes 8388608
  144.0 2.2 copy-start.7
  352.7 3.6 copy-start.1

commit v2 on v1

--- a/solution.py
+++ b/solution.py
@@ -13,6 +13,7 @@
 epsilon = 1e-06
 SUB = 8
 LANES = 256
+LAG = 3
 
 
 def flip(v, w):
@@ -201,9 +202,9 @@
 
 
 def mlp_kernel(
-    a_ref, b_ref, zc_ref, xp_ref, dy_ref, carry_ref, wo_ref, wu_ref, wd_ref,
+    a_ref, b_ref, zc_ref, xp_ref, nt_ref, dy_ref, carry_ref, wo_ref, wu_ref, wd_ref,
     obias_ref, gain_ref, ubias_ref, dbias_ref,
-    s_ref, sb_ref, act_ref, gu_ref, dyt_ref, n2t_ref, grt_ref, gres_ref, gs_ref, result_ref,
+    s_ref, acts_ref, gu_ref, rows_ref, turned_ref, gres_ref, gs_ref, result_ref,
     mu_ref, gdb_ref, gub_ref, ggain_ref, gob_ref,
     state, prod, perm,
 ):
@@ -224,15 +225,18 @@
         s_ref[sl, :] = st
     state[...] = st
     sb = s_ref[...].astype(BF16)
-    sb_ref[...] = sb
+    ff = wu_ref.shape[1]
+    acts_ref[:, ff:] = sb
     source = xp_ref[...].astype(F32)
     resid = source + dot(sb, wo_ref[...]) + obias_ref[...]
     scale = inv_rms(resid)
     n2 = (resid * scale * gain_ref[...]).astype(BF16)
-    n2t_ref[...] = n2.T
+    half = turned_ref.shape[2]
+    turned_ref[0] = n2.T.reshape(-1, half, n2.shape[0])
+    turned_ref[1] = nt_ref[...].reshape(-1, half, n2.shape[0])
     dy32 = to_steps(dy_ref[...], perm)
     dy = dy32.astype(BF16)
-    dyt_ref[...] = dy.T
+    rows_ref[0] = dy
     gdb_ref[...] += fold_rows(dy32)
     down = None
     gn2 = None
@@ -241,7 +245,7 @@
         upper = dot(n2, wu_ref[:, cols]) + ubias_ref[:, cols]
         act, slope = gelu_parts(upper)
         act = act.astype(BF16)
-        act_ref[:, cols] = act
+        acts_ref[:, cols] = act
         gact = dot_t(dy, wd_ref[cols, :])
         gu = (gact * slope).astype(BF16)
         gu_ref[:, cols] = gu
@@ -260,7 +264,7 @@
     gres_ref[...] = gres
     gr = gres.astype(BF16)
     gob_ref[...] += fold_rows(gr.astype(F32))
-    grt_ref[...] = gr.T
+    rows_ref[1] = gr
     gs = dot_t(gr, wo_ref[...])
     gs_ref[...] = gs
     pr = prod[...]
@@ -273,56 +277,6 @@
     mu_ref[...] = mu
 
 
-def back_kernel(
-    a_ref, b_ref, zc_ref, fc_ref, ic_ref, s_ref, gs_ref, xp_ref, gres_ref, carry_ref, wg_ref,
-    gain_ref,
-    gm_ref, gin_ref, ggb_ref, ggain_ref,
-    state, perm,
-):
-    i = pl.program_id(0)
-    steps = gin_ref.shape[1]
-    hid = wg_ref.shape[1] // 3
-
-    @pl.when(i == 0)
-    def _():
-        state[...] = carry_ref[...]
-        for ref in (ggb_ref, ggain_ref):
-            ref[...] = jnp.zeros_like(ref)
-
-    gn = None
-    for j in range(hid // LANES):
-        here = slice(j * LANES, (j + 1) * LANES)
-        mu = state[:, here]
-        lams = [None] * steps
-        for r in range(steps - 1, -1, -1):
-            sl = slice(r * SUB, (r + 1) * SUB)
-            lams[r] = gs_ref[sl, here] + mu
-            mu = a_ref[sl, here] * lams[r]
-        state[:, here] = mu
-        lam = jnp.concatenate(lams, axis=0)
-        gzc = lam * b_ref[:, here]
-        big = gzc * (s_ref[:, here] - zc_ref[:, here])
-        parts = (
-            (big * fc_ref[:, here].astype(F32)).astype(BF16),
-            (-big * ic_ref[:, here].astype(F32)).astype(BF16),
-            gzc.astype(BF16),
-        )
-        for g in range(3):
-            cols = slice(g * hid + j * LANES, g * hid + (j + 1) * LANES)
-            gm_ref[:, cols] = parts[g]
-            ggb_ref[:, cols] += fold_rows(parts[g].astype(F32))
-            n = dot_t(parts[g], wg_ref[:, cols])
-            gn = n if gn is None else gn + n
-    source = xp_ref[...].astype(F32)
-    scale = inv_rms(source)
-    w = gn * gain_ref[...]
-    ggain_ref[...] += fold_rows(gn * source * scale)
-    gin = gres_ref[...] + scale * w - source * (scale * scale * scale) * jnp.mean(
-        w * source, axis=-1, keepdims=True
-    )
-    gin_ref[...] = from_steps(gin, perm, steps)
-
-
 def bits_of(size):
     w = 1
     out = []
@@ -334,7 +288,7 @@
     def __init__(self, seq, batch, rows):
         sb = [("seq", w) for w in bits_of(seq)]
         bb = [("batch", w) for w in bits_of(batch)][1:]
-        self.orders = [sb + bb, sb[::-1] + bb, bb[:1] + sb + bb[1:], sb + bb, sb[::-1] + bb, bb[:1] + sb[::-1] + bb[1:]]
+        self.orders = [sb + bb, sb[::-1] + bb, bb[:1] + sb + bb[1:]]
         self.K = len(sb) + len(bb)
         self.rows = rows
         self.sizes = [rows]
@@ -434,17 +388,6 @@
             else:
                 done(c)
 
-def greet(plan, extra=()):
-    s = lax.axis_index("seq"); b = lax.axis_index("batch")
-    who = [(s, flip(b, 1))]
-    for axis, w in plan.orders[0]:
-        who.append((flip(s, w), b) if axis == "seq" else (s, flip(b, w)))
-    who += list(extra)
-    bar = pltpu.get_barrier_semaphore()
-    for p in who:
-        pl.semaphore_signal(bar, inc=1, device_id=p, device_id_type=MESH)
-    pl.semaphore_wait(bar, len(who))
-
 
 def small_copy(plan, small, got, ssem, rsem, k):
     _, dev = step_info(plan, k, 0)
@@ -453,60 +396,208 @@
         device_id=dev, device_id_type=MESH)
 
 
-def ar_kernel(plan, nchunks, lag, x_hbm, small_in, o_hbm, small_out,
-              acc, recv, ssem, rsem, free, isem, osem, small, got, s2sem, r2sem):
-    cp = pltpu.make_async_copy(x_hbm, acc, isem)
-    cp.start()
-    small[...] = small_in[...]
-    greet(plan)
-    cp.wait()
-    def out_copy(c):
-        rows = pl.ds(pl.multiple_of(c * plan.rows, 8), plan.rows)
-        return pltpu.make_async_copy(acc.at[rows], o_hbm.at[rows], osem.at[c])
-    def body(t, _):
-        for k in range(plan.K + 2):
-            @pl.when(t == k * lag)
+def tdot(a, b):
+    return lax.dot_general(a, b, (((0,), (0,)), ((), ())), preferred_element_type=F32)
+
+
+class Work:
+    def __init__(self, d, hid, ff, rows, tiles, lag, seq, batch):
+        self.rows = rows
+        self.halves = d // rows
+        self.down = ff // rows
+        self.up = ff // d * self.halves
+        self.out = hid // rows
+        self.gates = 3 * hid // d * self.halves
+        self.at_up = self.down
+        self.at_out = self.at_up + self.up
+        self.at_gates = self.at_out + self.out
+        self.chunks = self.at_gates + self.gates
+        self.plan = Plan(seq, batch, rows)
+        self.lag = lag
+        self.tiles = tiles
+        self.first_tile = 2
+        self.small_at = max(self.first_tile + tiles, self.at_gates)
+        self.ticks = max(self.chunks + lag * self.plan.stages, self.small_at + lag * (self.plan.K + 1)) + 1
+        self.seq = seq
+
+
+def back_tile(i, a_ref, b_ref, zc_ref, fc_ref, ic_ref, s_ref, gs_ref, xp_ref, gres_ref, wg_ref, gain_ref,
+              gin_ref, gm, ggb, ggain, state, perm):
+    steps = gin_ref.shape[1]
+    rows = steps * SUB
+    hid = wg_ref.shape[1] // 3
+    width = gm.shape[2]
+    at = pl.ds(pl.multiple_of(gm.shape[1] - (i + 1) * rows, rows), rows)
+    gn = None
+    for j in range(hid // LANES):
+        here = slice(j * LANES, (j + 1) * LANES)
+        mu = state[:, here]
+        lams = [None] * steps
+        for r in range(steps - 1, -1, -1):
+            sl = slice(r * SUB, (r + 1) * SUB)
+            lams[r] = gs_ref[sl, here] + mu
+            mu = a_ref[sl, here] * lams[r]
+        state[:, here] = mu
+        lam = jnp.concatenate(lams, axis=0)
+        gzc = lam * b_ref[:, here]
+        big = gzc * (s_ref[:, here] - zc_ref[:, here])
+        parts = (
+            (big * fc_ref[:, here].astype(F32)).astype(BF16),
+            (-big * ic_ref[:, here].astype(F32)).astype(BF16),
+            gzc.astype(BF16),
+        )
+        for g in range(3):
+            first = g * hid + j * LANES
+            cols = slice(first, first + LANES)
+            gm[first // width, at, first % width : first % width + LANES] = parts[g]
+            ggb[:, cols] += fold_rows(parts[g].astype(F32))
+            n = dot_t(parts[g], wg_ref[:, cols])
+            gn = n if gn is None else gn + n
+    source = xp_ref[...].astype(F32)
+    scale = inv_rms(source)
+    w = gn * gain_ref[...]
+    ggain[...] += fold_rows(gn * source * scale)
+    gin = gres_ref[...] + scale * w - source * (scale * scale * scale) * jnp.mean(
+        w * source, axis=-1, keepdims=True
+    )
+    gin_ref[...] = from_steps(gin, perm, steps)
+
+
+def sum_kernel(
+    work,
+    prod_ref, mu_ref, gdb_ref, gub_ref, ggain2_ref, gob_ref, gain_ref, wg_ref,
+    acts_ref, rows_ref, turned_ref, gu_ref,
+    a_ref, b_ref, zc_ref, fc_ref, ic_ref, s_ref, gs_ref, xp_ref, gres_ref,
+    gin_ref, small_ref, down_hbm, up_hbm, out_hbm, gates_hbm,
+    acc, recv, gm, state, ggb, ggain, perm, small, got, mine, theirs,
+    ssem, rsem, free, osem, s2sem, r2sem, csem, crsem,
+):
+    t = pl.program_id(0)
+    plan = work.plan
+    rows = work.rows
+    s = lax.axis_index("seq")
+    b = lax.axis_index("batch")
+    others = [lax.rem(s + k, work.seq) for k in range(1, work.seq)]
+    ends = [
+        pltpu.make_async_remote_copy(
+            src_ref=mine, dst_ref=theirs.at[k], send_sem=csem.at[k], recv_sem=crsem.at[k],
+            device_id=(others[k], b), device_id_type=MESH,
+        )
+        for k in range(work.seq - 1)
+    ]
+    width = prod_ref.shape[1]
+
+    @pl.when(t == 0)
+    def _():
+        who = [(s, flip(b, 1))] + [(o, b) for o in others]
+        who += [(s, flip(b, w)) for axis, w in plan.orders[0] if axis == "batch"]
+        bar = pltpu.get_barrier_semaphore()
+        for p in who:
+            pl.semaphore_signal(bar, inc=1, device_id=p, device_id_type=MESH)
+        prod = jnp.ones((1, width), F32)
+        total = jnp.zeros((1, width), F32)
+        for c in range(SUB - 1, -1, -1):
+            prod = prod * prod_ref[c : c + 1, :]
+            total = total * prod_ref[c : c + 1, :] + mu_ref[c : c + 1, :]
+        mine[0:1, :] = prod
+        mine[1:2, :] = total
+        ggb[...] = jnp.zeros_like(ggb)
+        ggain[...] = jnp.zeros_like(ggain)
+        pl.semaphore_wait(bar, len(who))
+        for c in ends:
+            c.start()
+
+    @pl.when(t == work.first_tile)
+    def _():
+        for c in ends:
+            c.wait()
+        now = jnp.zeros((1, width), F32)
+        for owner in range(work.seq - 1, 0, -1):
+            back = lax.rem(s - owner + work.seq, work.seq)
+            slot = jnp.where(back == 0, 0, back - 1)
+            new = theirs[slot, 0:1, :] * now + theirs[slot, 1:2, :]
+            now = jnp.where(owner > s, new, now)
+        for c in range(SUB - 1, -1, -1):
+            state[c : c + 1, :] = now
+            now = prod_ref[c : c + 1, :] * now + mu_ref[c : c + 1, :]
+
+    def put(value):
+        acc[pl.ds(pl.multiple_of(t * rows, rows), rows), :] = value
+
+    @pl.when((t < work.at_up) | ((t >= work.at_out) & (t < work.at_gates)))
+    def _():
+        put(tdot(acts_ref[...], rows_ref[0]))
+
+    @pl.when((t >= work.at_up) & (t < work.at_out))
+    def _():
+        put(dot(turned_ref[0], gu_ref[...]))
+
+    @pl.when((t >= work.at_gates) & (t < work.chunks))
+    def _():
+        put(dot(turned_ref[0], gm[(t - work.at_gates) // work.halves]))
+
+    @pl.when(t == work.small_at)
+    def _():
+        line = 0
+        for v in (ggain, ggb, gob_ref, ggain2_ref, gub_ref, gdb_ref):
+            total = jnp.sum(v[...], axis=0, keepdims=True)
+            for k in range(total.shape[1] // LANES):
+                small[line : line + 1, :] = total[:, k * LANES : (k + 1) * LANES]
+                line += 1
+        if line < small.shape[0]:
+            small[line:, :] = jnp.zeros((small.shape[0] - line, LANES), F32)
+
+    for k in range(plan.K + 2):
+        @pl.when(t == work.small_at + k * work.lag)
+        def _():
+            if k > 0:
+                small_copy(plan, small, got, s2sem, r2sem, k - 1).wait()
+                small[...] = small[...] + got[k - 1]
+            if k <= plan.K:
+                small_copy(plan, small, got, s2sem, r2sem, k).start()
+
+    d = rows * work.halves
+
+    def to_result(c, action):
+        src = acc.at[pl.ds(pl.multiple_of(c * rows, rows), rows)]
+
+        def case(first, count, ref, tall):
+            @pl.when((c >= first) & (c < first + count))
             def _():
-                if k > 0:
-                    small_copy(plan, small, got, s2sem, r2sem, k - 1).wait()
-                    small[...] = small[...] + got[k - 1]
-                if k <= plan.K:
-                    small_copy(plan, small, got, s2sem, r2sem, k).start()
-        tick(plan, nchunks, acc, recv, ssem, rsem, free, t, lambda c: out_copy(c).start(), lag)
-        return 0
-    lax.fori_loop(0, nchunks + lag * plan.stages, body, 0)
-    small_out[...] = small[...]
-    def wait(c, _):
-        out_copy(c).wait()
-        return 0
-    lax.fori_loop(0, nchunks, wait, 0)
-
-def all_reduce(x, small, seq, batch, chunk_rows, lag):
-    plan = Plan(seq, batch, chunk_rows)
-    n = x.shape[0] // chunk_rows
-    slots = plan.colors * 2
-    any_space = pl.BlockSpec(memory_space=pl.ANY)
-    vmem = pl.BlockSpec(memory_space=pltpu.VMEM)
-    return pl.pallas_call(
-        functools.partial(ar_kernel, plan, n, lag),
-        out_shape=[jax.ShapeDtypeStruct(x.shape, F32), jax.ShapeDtypeStruct(small.shape, F32)],
-        in_specs=[any_space, vmem],
-        out_specs=[any_space, vmem],
-        scratch_shapes=[
-            pltpu.VMEM(x.shape, F32),
-            pltpu.VMEM((slots, plan.recv_rows, x.shape[1]), F32),
-            pltpu.SemaphoreType.DMA((slots, plan.stages)),
-            pltpu.SemaphoreType.DMA((slots, plan.stages)),
-            pltpu.SemaphoreType.REGULAR((slots, plan.K + 1)),
-            pltpu.SemaphoreType.DMA,
-            pltpu.SemaphoreType.DMA((n,)),
-            pltpu.VMEM(small.shape, F32),
-            pltpu.VMEM((plan.K + 1,) + small.shape, F32),
-            pltpu.SemaphoreType.DMA((plan.K + 1,)),
-            pltpu.SemaphoreType.DMA((plan.K + 1,)),
-        ],
-        compiler_params=pltpu.CompilerParams(collective_id=0, has_side_effects=True, vmem_limit_bytes=60 << 20),
-    )(x, small)
+                k = c - first
+                if tall:
+                    dst = ref.at[pl.ds(pl.multiple_of(k * rows, rows), rows)]
+                else:
+                    dst = ref.at[
+                        pl.ds(pl.multiple_of((k % work.halves) * rows, rows), rows),
+                        pl.ds(pl.multiple_of((k // work.halves) * d, d), d),
+                    ]
+                action(pltpu.make_async_copy(src, dst, osem.at[c]))
+
+        case(0, work.down, down_hbm, True)
+        case(work.at_up, work.up, up_hbm, False)
+        case(work.at_out, work.out, out_hbm, True)
+        case(work.at_gates, work.gates, gates_hbm, False)
+
+    tick(plan, work.chunks, acc, recv, ssem, rsem, free, t,
+         lambda c: to_result(c, lambda copy: copy.start()), work.lag)
+
+    i = t - work.first_tile
+
+    @pl.when((i >= 0) & (i < work.tiles))
+    def _():
+        back_tile(i, a_ref, b_ref, zc_ref, fc_ref, ic_ref, s_ref, gs_ref, xp_ref, gres_ref, wg_ref,
+                  gain_ref, gin_ref, gm, ggb, ggain, state, perm)
+
+    @pl.when(t == work.ticks - 1)
+    def _():
+        small_ref[...] = small[...]
+
+        def wait(c, _):
+            to_result(c, lambda copy: copy.wait())
+            return 0
+
+        lax.fori_loop(0, work.chunks, wait, 0)
 
 
 def full(shape):
@@ -517,14 +608,15 @@
     return pl.BlockSpec(shape, lambda i: (0,) * len(shape))
 
 
-def local_part(mesh_seq, inputs, cotangent, short_lengths, long_lengths, norm_gain, w_gates, gate_bias, w_out,
-               out_bias, mlp_gain, w_up, up_bias, w_down, down_bias, tile=256):
+def per_device(seq, batch, inputs, cotangent, short_lengths, long_lengths, norm_gain, w_gates, gate_bias, w_out,
+               out_bias, mlp_gain, w_up, up_bias, w_down, down_bias, tile=256, back=128):
     tok, d = inputs.shape[1:]
     hid = w_out.shape[0]
     ff = w_up.shape[1]
     piece = tok // SUB
     steps = tile // SUB
     grid = tok // tile
+    halves = 2
     x = inputs.reshape(SUB, piece, d)
     dy = cotangent.reshape(SUB, piece, d)
     gain1 = norm_gain.reshape(1, d)
@@ -550,78 +642,96 @@
         compiler_params=params,
     )(short_lengths, long_lengths, x, gain1, w_gates, gate_bias.reshape(1, 3 * hid))
 
-    enter = carry(mesh_seq, False, prod, total)
+    enter = carry(seq, False, prod, total)
 
     outs = pl.pallas_call(
         mlp_kernel,
         grid=(grid,),
-        in_specs=[rows(hid)] * 3 + [rows(d), natural, full((SUB, hid)), full((hid, d)), full((d, ff)), full((ff, d)),
+        in_specs=[rows(hid)] * 3 + [rows(d), turned, natural, full((SUB, hid)), full((hid, d)), full((d, ff)), full((ff, d)),
                   full((1, d)), full((1, d)), full((1, ff)), full((1, d))],
-        out_specs=[rows(hid), rows(hid), rows(ff), rows(ff), turned, turned, turned, rows(d), rows(hid), natural,
+        out_specs=[rows(hid), rows(ff + hid), rows(ff), pl.BlockSpec((2, tile, d), lambda i: (0, i, 0)),
+                   pl.BlockSpec((2, halves, d // halves, tile), lambda i: (0, 0, 0, i)), rows(d), rows(hid), natural,
                    held((SUB, hid)), held((SUB, d)), held((SUB, ff)), held((SUB, d)), held((SUB, d))],
-        out_shape=[sds((tok, hid), F32), sds((tok, hid), BF16), sds((tok, ff), BF16), sds((tok, ff), BF16),
-                   sds((d, tok), BF16), sds((d, tok), BF16), sds((d, tok), BF16), sds((tok, d), F32),
+        out_shape=[sds((tok, hid), F32), sds((tok, ff + hid), BF16), sds((tok, ff), BF16), sds((2, tok, d), BF16),
+                   sds((2, halves, d // halves, tok), BF16), sds((tok, d), F32),
                    sds((tok, hid), F32), sds((SUB, piece, d), BF16),
                    sds((SUB, hid), F32), sds((SUB, d), F32), sds((SUB, ff), F32), sds((SUB, d), F32), sds((SUB, d), F32)],
         scratch_shapes=[pltpu.VMEM((SUB, hid), F32), pltpu.VMEM((SUB, hid), F32), pltpu.VMEM((d // 128, tile, 128), F32)],
         compiler_params=params,
-    )(a, b, zc, xp, dy, enter, w_out, w_up, w_down, out_bias.reshape(1, d), gain2, up_bias.reshape(1, ff),
+    )(a, b, zc, xp, nt, dy, enter, w_out, w_up, w_down, out_bias.reshape(1, d), gain2, up_bias.reshape(1, ff),
       down_bias.reshape(1, d))
-    s, sb, act, gu, dyt, n2t, grt, gres, gs, result, mu, gdb, gub, ggain2, gob = outs
-
-    enter_back = carry(mesh_seq, True, prod, mu)
-
-    back = lambda n: pl.BlockSpec((tile, n), lambda i: (grid - 1 - i, 0))
-    gm, gin, ggb, ggain1 = pl.pallas_call(
-        back_kernel,
-        grid=(grid,),
-        in_specs=[back(hid)] * 7 + [back(d), back(d), full((SUB, hid)), full((d, 3 * hid)), full((1, d))],
-        out_specs=[back(3 * hid), pl.BlockSpec((SUB, steps, d), lambda i: (0, grid - 1 - i, 0)),
-                   held((SUB, 3 * hid)), held((SUB, d))],
-        out_shape=[sds((tok, 3 * hid), BF16), sds((SUB, piece, d), F32), sds((SUB, 3 * hid), F32), sds((SUB, d), F32)],
-        scratch_shapes=[pltpu.VMEM((SUB, hid), F32), pltpu.VMEM((d // 128, tile, 128), F32)],
-        compiler_params=params,
-    )(a, b, zc, fc, ic, s, gs, xp, gres, enter_back, w_gates, gain1)
-    return (result, gin, (nt, gm), (grt, sb), (n2t, gu), (dyt, act),
-            (ggain1, ggb, gob, ggain2, gub, gdb))
-
-
-def blocks_of(v):
-    d, n = v.shape
-    return v.reshape(d, n // LANES, LANES).transpose(1, 0, 2).reshape(-1, LANES)
-
-
-def unblock(v, d):
-    n = v.shape[0] // d
-    return v.reshape(n, d, LANES).transpose(1, 0, 2).reshape(d, n * LANES)
-
-
-def per_device(seq, batch, *args):
-    result, gin, gates, out, up, down, small = local_part(seq, *args)
-    inputs = args[0]
-    d = inputs.shape[2]
-    big = [dot(*pair) for pair in (down, up, out, gates)]
-    vecs = [jnp.sum(v, axis=0) for v in small]
-    flat = jnp.concatenate(vecs)
-    lines = -(-flat.shape[0] // (8 * LANES)) * 8
-    flat = jnp.pad(flat, (0, lines * LANES - flat.shape[0])).reshape(lines, LANES)
-    total, flat = all_reduce(jnp.concatenate([blocks_of(v) for v in big]), flat, seq, batch, d, 3)
-    flat = flat.reshape(-1)
-    grads = []
+    s, acts, gu, pairs, turns, gres, gs, result, mu, gdb, gub, ggain2, gob = outs
+
+    turns = turns.reshape(2 * halves, d // halves, tok)
+    work = Work(d, hid, ff, d // halves, tok // back, LAG, seq, batch)
+    plan = work.plan
+    slots = plan.colors * 2
+    bsteps = back // SUB
+    lines = -(-(4 * d + 3 * hid + ff) // (8 * LANES)) * 8
+
+    def at_tile(t):
+        return work.tiles - 1 - jnp.clip(t - work.first_tile, 0, work.tiles - 1)
+
+    btile = lambda n: pl.BlockSpec((back, n), lambda t: (at_tile(t), 0))
+    any_space = pl.BlockSpec(memory_space=pl.ANY)
+
+    def acts_at(t):
+        late = jnp.clip(t - work.up, work.down, work.down + work.out - 1)
+        return (0, jnp.where(t < work.down, t, late))
+
+    def turned_at(t):
+        up = jnp.clip(t - work.at_up, 0, work.up - 1) % halves
+        gates = halves + jnp.clip(t - work.at_gates, 0, work.gates - 1) % halves
+        return (jnp.where(t < work.at_out, up, gates), 0, 0)
+
+    gin, small, g_down, g_up, g_out, g_gates = pl.pallas_call(
+        functools.partial(sum_kernel, work),
+        grid=(work.ticks,),
+        in_specs=[full((SUB, hid)), full((SUB, hid)), full((SUB, d)), full((SUB, ff)), full((SUB, d)), full((SUB, d)),
+                  full((1, d)), full((d, 3 * hid)),
+                  pl.BlockSpec((tok, work.rows), acts_at),
+                  pl.BlockSpec((1, tok, d), lambda t: (jnp.where(t < work.at_up, 0, 1), 0, 0)),
+                  pl.BlockSpec((1, work.rows, tok), turned_at),
+                  pl.BlockSpec((tok, d), lambda t: (0, jnp.clip(t - work.at_up, 0, work.up - 1) // halves))]
+        + [btile(hid)] * 7 + [btile(d)] * 2,
+        out_specs=[pl.BlockSpec((SUB, bsteps, d), lambda t: (0, at_tile(t), 0)), held((lines, LANES))] + [any_space] * 4,
+        out_shape=[sds((SUB, piece, d), F32), sds((lines, LANES), F32), sds((ff, d), F32), sds((d, ff), F32),
+                   sds((hid, d), F32), sds((d, 3 * hid), F32)],
+        scratch_shapes=[
+            pltpu.VMEM((work.chunks * work.rows, d), F32),
+            pltpu.VMEM((slots, plan.recv_rows, d), F32),
+            pltpu.VMEM((3 * hid // d, tok, d), BF16),
+            pltpu.VMEM((SUB, hid), F32),
+            pltpu.VMEM((SUB, 3 * hid), F32),
+            pltpu.VMEM((SUB, d), F32),
+            pltpu.VMEM((d // 128, back, 128), F32),
+            pltpu.VMEM((lines, LANES), F32),
+            pltpu.VMEM((plan.K + 1, lines, LANES), F32),
+            pltpu.VMEM((SUB, hid), F32),
+            pltpu.VMEM((seq - 1, SUB, hid), F32),
+            pltpu.SemaphoreType.DMA((slots, plan.stages)),
+            pltpu.SemaphoreType.DMA((slots, plan.stages)),
+            pltpu.SemaphoreType.REGULAR((slots, plan.K + 1)),
+            pltpu.SemaphoreType.DMA((work.chunks,)),
+            pltpu.SemaphoreType.DMA((plan.K + 1,)),
+            pltpu.SemaphoreType.DMA((plan.K + 1,)),
+            pltpu.SemaphoreType.DMA((seq - 1,)),
+            pltpu.SemaphoreType.DMA((seq - 1,)),
+        ],
+        compiler_params=pltpu.CompilerParams(
+            dimension_semantics=("arbitrary",), collective_id=0, has_side_effects=True, vmem_limit_bytes=62 << 20
+        ),
+    )(prod, mu, gdb, gub, ggain2, gob, gain1, w_gates, acts, pairs, turns, gu,
+      a, b, zc, fc, ic, s, gs, xp, gres)
+    small = small.reshape(-1)
+    vecs = []
     at = 0
-    for v in big:
-        n = v.shape[1] // LANES * d
-        grads.append(unblock(total[at : at + n], d))
+    for n in (d, 3 * hid, d, d, ff, d):
+        vecs.append(small[at : at + n])
         at += n
-    svecs = []
-    at = 0
-    for v in vecs:
-        svecs.append(flat[at : at + v.shape[0]])
-        at += v.shape[0]
-    g_down, g_up, g_out, g_gates = grads
-    ggain1, ggb, gob, ggain2, gub, gdb = svecs
-    return (result.reshape(inputs.shape), gin.reshape(inputs.shape), ggain1, g_gates, ggb, g_out.T, gob,
-            ggain2, g_up, gub, g_down.T, gdb)
+    ggain1, ggb, gob, ggain2, gub, gdb = vecs
+    return (result.reshape(inputs.shape), gin.reshape(inputs.shape), ggain1, g_gates, ggb, g_out, gob,
+            ggain2, g_up, gub, g_down, gdb)
 
 
 def solution(mesh):

time: 361 us -> 273 us (0.76)
  local copies, waits for them, and re-layouts: 62.9 us -> 23.7 us
  matrix products: 22.8 us -> 0 us
  other arithmetic: 16 us -> 0 us
  Pallas kernels: 257 us -> 249 us
    dot_general x4 -> x0, matrix products: 22.8 us -> none  [dot(): return jnp.dot(a, b, preferred_element_type=F32)]
    reshape x6 -> x0, local copies, waits for them, and re-layouts: 17.3 us -> none  [the longest x2 11.4 us: unblock(): return v.reshape(n, d, LANES).transpose(1, 0, 2).reshape(d, n * LANES)]
    concatenate x1 -> x0, other arithmetic: 14.2 us -> none  [per_device(): jnp.concatenate([blocks_of(v) for v in big])]
    slice x5 -> x2, local copies, waits for them, and re-layouts: 15.5 us -> 1.34 us  [per_device(): vecs.append(small[at:at + n])]
    transpose x3 -> x0, local copies, waits for them, and re-layouts: 13.7 us -> none  [the longest x2 7.15 us: unblock(): return v.reshape(n, d, LANES).transpose(1, 0, 2).reshape(d, n * LANES)]
    pallas_call x2 -> x1, Pallas kernels: 14.8 us -> 8.18 us  [carry(): pl.pallas_call(functools.partial(carry_kernel, devices, reverse), out_sha...]
    unnamed x42 -> x21, local copies, waits for them, and re-layouts: 16.3 us -> 22.3 us
    pallas_call x4 -> x3, Pallas kernels: 242 us -> 240 us  [the longest x1 167 us: per_device(): pl.pallas_call(functools.partial(sum_kernel, work), grid=(work.ticks,), i...]
where the time goes in v2:
time: 273 us
  Pallas kernels  249 us (91%)
  local copies, waits for them, and re-layouts  23.7 us (9%)
    pallas_call x1, Pallas kernels, per_device(): pl.pallas_call(functools.partial(sum_kernel, work), grid=(work.ticks,), i...  167 us
    pallas_call x1, Pallas kernels, per_device(): pl.pallas_call(mlp_kernel, grid=(grid,), in_specs=[rows(hid)] * 3 + [rows...  53 us
    unnamed x21, local copies, waits for them, and re-layouts  22.3 us
    pallas_call x1, Pallas kernels, per_device(): pl.pallas_call(functools.partial(gates_kernel, piece), grid=(grid,), in_s...  20.4 us
    pallas_call x1, Pallas kernels, carry(): pl.pallas_call(functools.partial(carry_kernel, devices, reverse), out_sha...  8.18 us

profile of v2, /device:TPU:0, one launch (start us, length us, event | category | flops | bytes accessed | tf_op | source)
XLA Modules:
  0.0 273.0 jit_solution(2754054050730217753)
XLA Ops:
  0.6 1.3 copy.26.long_ref
  2.0 20.4 %shard_map.229 = (f32[2048,1024]{1,0:T(8,128)}, f32[2048,1024]{1,0:T(8,128)}, f32[2048,1024]{1,0:T(8,128)}, bf16[2048,1024]{1,0:T(8,128)(2,1)}, bf16[2048,1024]{...) custom-call(s32[4,4]{1,0:T(4,128)} %short_ref.1, ...), custom_call_target="tpu_custom_call" | custom-call | tf_op jit(solution)/shard_map/pallas_call | solution.py:631
  22.4 8.2 %shard_map.230.carry_ref = f32[8,1024]{1,0:T(8,128)} custom-call(f32[8,1024]{1,0:T(8,128)} %get-tuple-element.45.prod_ref, f32[8,1024]{1,0:T(8,128)} %get-tuple-element.46.sum_ref), custom_call_target="tpu_custom_call" | custom-call | tf_op jit(solution)/shard_map/pallas_call | solution.py:173
  30.6 53.0 %shard_map.231 = (f32[2048,1024]{1,0:T(8,128)}, bf16[2048,3072]{1,0:T(8,128)(2,1)}, bf16[2048,2048]{1,0:T(8,128)(2,1)}, bf16[2,2048,512]{2,1,0:T(8,128)(2,1)}, b...) custom-call(f32[2048,1024]{1,0:T(8,128)} %get-tuple-element.40.a_ref, ...), custom_call_target="tpu_custom_call" | custom-call | tf_op jit(solution)/shard_map/pallas_call | solution.py:647
  83.6 167.0 %shard_map.232 = (f32[8,256,512]{2,1,0:T(8,128)}, f32[32,256]{1,0:T(8,128)}, f32[2048,512]{1,0:T(8,128)}, f32[512,2048]{1,0:T(8,128)}, f32[1024,512]{1,0:T(8,128)}, /*index=5*/f32[512,3072]{1,0:T(8,128)}) custom-call(f32[8,1024]{1,0:T(8,128)} %get-tuple-element.45.prod_ref, f32[8,1024]{1,0:T(8,128)} %get-tuple-element.48.mu_ref, ...), custom_call_target="tpu_custom_call" | custom-call | tf_op jit(solution)/shard_map/pallas_call | solution.py:687
  250.6 0.8 slice_bitcast_fusion.1
  251.4 0.6 copy.27
  252.0 0.7 slice.38
  252.7 0.6 slice.39
  253.3 0.6 copy.28
  253.9 0.6 copy.29
  254.5 0.7 slice_bitcast_fusion
  255.2 0.6 copy.30
  255.8 0.6 copy.31
  256.4 0.0 copy-start
  256.4 4.8 %copy.37 = f32[1,2048,512]{2,1,0:T(8,128)} copy(f32[1,2048,512]{2,1,0:T(8,128)} %bitcast.27) | data formatting | bytes 8388608
  261.2 0.0 copy-done
  261.2 0.0 copy-start.3
  261.2 2.8 %copy.38 = f32[512,3072]{1,0:T(8,128)} copy(f32[512,3072]{1,0:T(8,128)S(1)} %copy-done) | data formatting | bytes 12582912
  264.0 0.3 copy-done.3
  264.3 0.0 copy-start.2
  264.3 1.3 copy.39
  265.6 1.6 copy-done.2
  267.3 0.0 copy-start.1
  267.3 2.1 copy.40
  269.4 1.6 copy-done.1
  271.0 2.0 copy.41
Async XLA Ops:
  256.4 4.8 %copy-start = (f32[512,3072]{1,0:T(8,128)S(1)}, f32[512,3072]{1,0:T(8,128)}, u32[]{:S(2)}) copy-start(f32[512,3072]{1,0:T(8,128)} %get-tuple-element.87) | copy-start | bytes 18874372
  261.2 3.1 %copy-start.3 = (f32[1024,512]{1,0:T(8,128)S(1)}, f32[1024,512]{1,0:T(8,128)}, u32[]{:S(2)}) copy-start(f32[1024,512]{1,0:T(8,128)} %get-tuple-element.89) | copy-start | bytes 6291460
  264.3 2.9 %copy-start.2 = (f32[512,2048]{1,0:T(8,128)S(1)}, f32[512,2048]{1,0:T(8,128)}, u32[]{:S(2)}) copy-start(f32[512,2048]{1,0:T(8,128)} %get-tuple-element.92) | copy-start | bytes 12582916
  267.3 3.7 %copy-start.1 = (f32[2048,512]{1,0:T(8,128)S(1)}, f32[2048,512]{1,0:T(8,128)}, u32[]{:S(2)}) copy-start(f32[2048,512]{1,0:T(8,128)} %get-tuple-element.94) | copy-start | bytes 12582916

commit v3 on v2

--- a/solution.py
+++ b/solution.py
@@ -41,9 +41,14 @@
     flat = block.astype(F32).reshape(pieces * steps, n)
     parts = []
     for k in range(n // 128):
-        scratch[k] = flat[:, k * 128 : (k + 1) * 128]
+        for c in range(pieces):
+            scratch[k, c * (steps + SUB) : c * (steps + SUB) + steps, :] = flat[
+                c * steps : (c + 1) * steps, k * 128 : (k + 1) * 128
+            ]
         parts.append(
-            jnp.concatenate([scratch[k, pl.ds(r, pieces, stride=steps), :] for r in range(steps)], axis=0)
+            jnp.concatenate(
+                [scratch[k, pl.ds(r, pieces, stride=steps + SUB), :] for r in range(steps)], axis=0
+            )
         )
     return jnp.concatenate(parts, axis=1)
 
@@ -53,18 +58,81 @@
     parts = []
     for k in range(n // 128):
         for r in range(steps):
-            scratch[k, pl.ds(r, SUB, stride=steps), :] = value[
+            scratch[k, pl.ds(r, SUB, stride=steps + SUB), :] = value[
                 r * SUB : (r + 1) * SUB, k * 128 : (k + 1) * 128
             ]
-        parts.append(scratch[k])
+        parts.append(
+            jnp.concatenate(
+                [scratch[k, c * (steps + SUB) : c * (steps + SUB) + steps, :] for c in range(SUB)], axis=0
+            )
+        )
     return jnp.concatenate(parts, axis=1).reshape(SUB, steps, n)
 
 
+class Ends:
+    def __init__(self, devices, mine, theirs, ssem, rsem):
+        self.devices = devices
+        self.mine = mine
+        self.theirs = theirs
+        self.at = lax.axis_index("seq")
+        self.group = lax.axis_index("batch")
+        self.others = [lax.rem(self.at + k, devices) for k in range(1, devices)]
+        self.copies = [
+            pltpu.make_async_remote_copy(
+                src_ref=mine, dst_ref=theirs.at[k], send_sem=ssem.at[k], recv_sem=rsem.at[k],
+                device_id=(other, self.group), device_id_type=MESH,
+            )
+            for k, other in enumerate(self.others)
+        ]
+
+    def greet(self):
+        bar = pltpu.get_barrier_semaphore()
+        for other in self.others:
+            pl.semaphore_signal(bar, inc=1, device_id=(other, self.group), device_id_type=MESH)
+
+    def send(self, prod_ref, sum_ref, reverse):
+        width = prod_ref.shape[1]
+        prod = jnp.ones((1, width), F32)
+        total = jnp.zeros((1, width), F32)
+        for c in range(SUB - 1, -1, -1) if reverse else range(SUB):
+            prod = prod * prod_ref[c : c + 1, :]
+            total = total * prod_ref[c : c + 1, :] + sum_ref[c : c + 1, :]
+        self.mine[0:1, :] = prod
+        self.mine[1:2, :] = total
+        for copy in self.copies:
+            copy.start()
+
+    def receive(self, prod_ref, sum_ref, out_ref, reverse):
+        for copy in self.copies:
+            copy.wait()
+        n = self.devices
+        now = jnp.zeros((1, prod_ref.shape[1]), F32)
+        for owner in range(n - 1, 0, -1) if reverse else range(n - 1):
+            back = lax.rem(self.at - owner + n, n)
+            slot = jnp.where(back == 0, 0, back - 1)
+            new = self.theirs[slot, 0:1, :] * now + self.theirs[slot, 1:2, :]
+            now = jnp.where(owner > self.at if reverse else owner < self.at, new, now)
+        for c in range(SUB - 1, -1, -1) if reverse else range(SUB):
+            out_ref[c : c + 1, :] = now
+            now = prod_ref[c : c + 1, :] * now + sum_ref[c : c + 1, :]
+
+
+def ends_scratch(devices, width):
+    return [
+        pltpu.VMEM((SUB, width), F32),
+        pltpu.VMEM((devices - 1, SUB, width), F32),
+        pltpu.SemaphoreType.DMA((devices - 1,)),
+        pltpu.SemaphoreType.DMA((devices - 1,)),
+    ]
+
+
 def gates_kernel(
-    piece, short_ref, long_ref, x_ref, gain_ref, wg_ref, bias_ref,
-    a_ref, b_ref, zc_ref, fc_ref, ic_ref, xp_ref, nt_ref, prod_ref, sum_ref, perm,
+    piece, devices, short_ref, long_ref, x_ref, gain_ref, wg_ref, bias_ref,
+    a_ref, b_ref, zc_ref, fc_ref, ic_ref, xp_ref, nt_ref, prod_ref, enter_ref,
+    perm, sum_ref, mine, theirs, ssem, rsem,
 ):
     i = pl.program_id(0)
+    ends = Ends(devices, mine, theirs, ssem, rsem)
     steps = x_ref.shape[1]
     rows = steps * SUB
     hid = wg_ref.shape[1] // 3
@@ -94,6 +162,7 @@
 
     @pl.when(i == 0)
     def _():
+        ends.greet()
         prod_ref[...] = jnp.ones_like(prod_ref)
         sum_ref[...] = jnp.zeros_like(sum_ref)
 
@@ -122,69 +191,11 @@
         sum_ref[:, here] = total
 
 
-def carry_kernel(devices, reverse, prod_ref, sum_ref, out_ref, mine, got, ssem, rsem):
-    s = lax.axis_index("seq")
-    b = lax.axis_index("batch")
-    bar = pltpu.get_barrier_semaphore()
-    others = [lax.rem(s + k, devices) for k in range(1, devices)]
-    for o in others:
-        pl.semaphore_signal(bar, inc=1, device_id=(o, b), device_id_type=MESH)
-    order = list(range(SUB))[::-1] if reverse else list(range(SUB))
-    width = prod_ref.shape[1]
-    prod = jnp.ones((1, width), F32)
-    total = jnp.zeros((1, width), F32)
-    for c in order:
-        prod = prod * prod_ref[c : c + 1, :]
-        total = total * prod_ref[c : c + 1, :] + sum_ref[c : c + 1, :]
-    mine[0:1, :] = prod
-    mine[1:2, :] = total
-    pl.semaphore_wait(bar, devices - 1)
-    copies = []
-    for k in range(1, devices):
-        copies.append(
-            pltpu.make_async_remote_copy(
-                src_ref=mine, dst_ref=got.at[k - 1], send_sem=ssem.at[k - 1], recv_sem=rsem.at[k - 1],
-                device_id=(others[k - 1], b), device_id_type=MESH,
-            )
-        )
-        copies[-1].start()
-    for c in copies:
-        c.wait()
-    state = jnp.zeros((1, width), F32)
-    for turn in range(devices - 1):
-        if reverse:
-            owner = devices - 1 - turn
-            ahead = owner > s
-            back = lax.rem(s - owner + devices, devices)
-        else:
-            owner = turn
-            ahead = owner < s
-            back = lax.rem(s - owner + devices, devices)
-        slot = jnp.where(back == 0, 0, back - 1)
-        new = got[slot, 0:1, :] * state + got[slot, 1:2, :]
-        state = jnp.where(ahead, new, state)
-    for c in order:
-        out_ref[c : c + 1, :] = state
-        state = prod_ref[c : c + 1, :] * state + sum_ref[c : c + 1, :]
-
-
-def carry(devices, reverse, prod, total):
-    width = prod.shape[1]
-    return pl.pallas_call(
-        functools.partial(carry_kernel, devices, reverse),
-        out_shape=jax.ShapeDtypeStruct((SUB, width), F32),
-        in_specs=[pl.BlockSpec(memory_space=pltpu.VMEM)] * 2,
-        out_specs=pl.BlockSpec(memory_space=pltpu.VMEM),
-        scratch_shapes=[
-            pltpu.VMEM((SUB, width), F32),
-            pltpu.VMEM((devices - 1, SUB, width), F32),
-            pltpu.SemaphoreType.DMA((devices - 1,)),
-            pltpu.SemaphoreType.DMA((devices - 1,)),
-        ],
-        compiler_params=pltpu.CompilerParams(
-            collective_id=1 + int(reverse), has_side_effects=True
-        ),
-    )(prod, total)
+    @pl.when(i == pl.num_programs(0) - 1)
+    def _():
+        pl.semaphore_wait(pltpu.get_barrier_semaphore(), devices - 1)
+        ends.send(prod_ref, sum_ref, False)
+        ends.receive(prod_ref, sum_ref, enter_ref, False)
 
 
 KA = 0.3275911 * 2.0**-0.5
@@ -250,10 +261,8 @@
         gu = (gact * slope).astype(BF16)
         gu_ref[:, cols] = gu
         gub_ref[:, cols] += fold_rows(gu.astype(F32))
-        d = dot(act, wd_ref[cols, :])
-        n = dot_t(gu, wu_ref[:, cols])
-        down = d if down is None else down + d
-        gn2 = n if gn2 is None else gn2 + n
+    down = dot(acts_ref[:, :ff], wd_ref[...])
+    gn2 = dot_t(gu_ref[...], wu_ref[...])
     result = resid + down + dbias_ref[...]
     result_ref[...] = from_steps(result, perm, steps).astype(BF16)
     w = gn2 * gain_ref[...]
@@ -284,11 +293,15 @@
         out.append(w); w *= 2
     return out
 
+def stage_ticks(j, stages):
+    return LAG
+
+
 class Plan:
     def __init__(self, seq, batch, rows):
         sb = [("seq", w) for w in bits_of(seq)]
         bb = [("batch", w) for w in bits_of(batch)][1:]
-        self.orders = [sb + bb, sb[::-1] + bb, bb[:1] + sb + bb[1:]]
+        self.orders = [sb + bb, sb[::-1] + bb, bb[:1] + sb + bb[1:], sb + bb, sb[::-1] + bb, bb[:1] + sb[::-1] + bb[1:]]
         self.K = len(sb) + len(bb)
         self.rows = rows
         self.sizes = [rows]
@@ -299,6 +312,9 @@
             self.sizes.append(self.sizes[-1] // 2 if h else self.sizes[-1])
         self.stages = 2 * (self.K + 1)
         self.colors = len(self.orders)
+        self.begins = [0]
+        for j in range(self.stages):
+            self.begins.append(self.begins[-1] + stage_ticks(j, self.stages))
         self.base = []
         tot = 0
         for k in range(self.K + 1):
@@ -370,9 +386,9 @@
         off = offsets(plan, c, color, j + 1)
         acc[pl.ds(off, n), :] = acc[pl.ds(off, n), :] + recv[slot, pl.ds(plan.base[j], n), :]
 
-def tick(plan, nchunks, acc, recv, ssem, rsem, free, t, done, L=1):
+def tick(plan, nchunks, acc, recv, ssem, rsem, free, t, done):
     for j in range(plan.stages, -1, -1):
-        c = t - L * j
+        c = t - plan.begins[j]
         @pl.when((c >= 0) & (c < nchunks))
         def _():
             if j > 0:
@@ -417,18 +433,18 @@
         self.tiles = tiles
         self.first_tile = 2
         self.small_at = max(self.first_tile + tiles, self.at_gates)
-        self.ticks = max(self.chunks + lag * self.plan.stages, self.small_at + lag * (self.plan.K + 1)) + 1
+        self.ticks = max(self.chunks + self.plan.begins[-1], self.small_at + lag * (self.plan.K + 1)) + 1
+        self.steps = max(self.chunks, self.small_at) + 1
         self.seq = seq
 
 
 def back_tile(i, a_ref, b_ref, zc_ref, fc_ref, ic_ref, s_ref, gs_ref, xp_ref, gres_ref, wg_ref, gain_ref,
-              gin_ref, gm, ggb, ggain, state, perm):
+              gin_ref, gm, gmt, ggb, ggain, state, perm):
     steps = gin_ref.shape[1]
     rows = steps * SUB
     hid = wg_ref.shape[1] // 3
     width = gm.shape[2]
     at = pl.ds(pl.multiple_of(gm.shape[1] - (i + 1) * rows, rows), rows)
-    gn = None
     for j in range(hid // LANES):
         here = slice(j * LANES, (j + 1) * LANES)
         mu = state[:, here]
@@ -450,9 +466,9 @@
             first = g * hid + j * LANES
             cols = slice(first, first + LANES)
             gm[first // width, at, first % width : first % width + LANES] = parts[g]
+            gmt[:, cols] = parts[g]
             ggb[:, cols] += fold_rows(parts[g].astype(F32))
-            n = dot_t(parts[g], wg_ref[:, cols])
-            gn = n if gn is None else gn + n
+    gn = dot_t(gmt[...], wg_ref[...])
     source = xp_ref[...].astype(F32)
     scale = inv_rms(source)
     w = gn * gain_ref[...]
@@ -468,8 +484,8 @@
     prod_ref, mu_ref, gdb_ref, gub_ref, ggain2_ref, gob_ref, gain_ref, wg_ref,
     acts_ref, rows_ref, turned_ref, gu_ref,
     a_ref, b_ref, zc_ref, fc_ref, ic_ref, s_ref, gs_ref, xp_ref, gres_ref,
-    gin_ref, small_ref, down_hbm, up_hbm, out_hbm, gates_hbm,
-    acc, recv, gm, state, ggb, ggain, perm, small, got, mine, theirs,
+    gin_ref, small_ref, sums_hbm,
+    acc, recv, gm, gmt, state, ggb, ggain, perm, small, got, mine, theirs,
     ssem, rsem, free, osem, s2sem, r2sem, csem, crsem,
 ):
     t = pl.program_id(0)
@@ -477,49 +493,23 @@
     rows = work.rows
     s = lax.axis_index("seq")
     b = lax.axis_index("batch")
-    others = [lax.rem(s + k, work.seq) for k in range(1, work.seq)]
-    ends = [
-        pltpu.make_async_remote_copy(
-            src_ref=mine, dst_ref=theirs.at[k], send_sem=csem.at[k], recv_sem=crsem.at[k],
-            device_id=(others[k], b), device_id_type=MESH,
-        )
-        for k in range(work.seq - 1)
-    ]
-    width = prod_ref.shape[1]
+    ends = Ends(work.seq, mine, theirs, csem, crsem)
 
     @pl.when(t == 0)
     def _():
-        who = [(s, flip(b, 1))] + [(o, b) for o in others]
+        who = [(s, flip(b, 1))] + [(o, b) for o in ends.others]
         who += [(s, flip(b, w)) for axis, w in plan.orders[0] if axis == "batch"]
         bar = pltpu.get_barrier_semaphore()
         for p in who:
             pl.semaphore_signal(bar, inc=1, device_id=p, device_id_type=MESH)
-        prod = jnp.ones((1, width), F32)
-        total = jnp.zeros((1, width), F32)
-        for c in range(SUB - 1, -1, -1):
-            prod = prod * prod_ref[c : c + 1, :]
-            total = total * prod_ref[c : c + 1, :] + mu_ref[c : c + 1, :]
-        mine[0:1, :] = prod
-        mine[1:2, :] = total
         ggb[...] = jnp.zeros_like(ggb)
         ggain[...] = jnp.zeros_like(ggain)
         pl.semaphore_wait(bar, len(who))
-        for c in ends:
-            c.start()
+        ends.send(prod_ref, mu_ref, True)
 
     @pl.when(t == work.first_tile)
     def _():
-        for c in ends:
-            c.wait()
-        now = jnp.zeros((1, width), F32)
-        for owner in range(work.seq - 1, 0, -1):
-            back = lax.rem(s - owner + work.seq, work.seq)
-            slot = jnp.where(back == 0, 0, back - 1)
-            new = theirs[slot, 0:1, :] * now + theirs[slot, 1:2, :]
-            now = jnp.where(owner > s, new, now)
-        for c in range(SUB - 1, -1, -1):
-            state[c : c + 1, :] = now
-            now = prod_ref[c : c + 1, :] * now + mu_ref[c : c + 1, :]
+        ends.receive(prod_ref, mu_ref, state, True)
 
     def put(value):
         acc[pl.ds(pl.multiple_of(t * rows, rows), rows), :] = value
@@ -547,57 +537,85 @@
         if line < small.shape[0]:
             small[line:, :] = jnp.zeros((small.shape[0] - line, LANES), F32)
 
-    for k in range(plan.K + 2):
-        @pl.when(t == work.small_at + k * work.lag)
-        def _():
-            if k > 0:
-                small_copy(plan, small, got, s2sem, r2sem, k - 1).wait()
-                small[...] = small[...] + got[k - 1]
-            if k <= plan.K:
-                small_copy(plan, small, got, s2sem, r2sem, k).start()
-
+    def to_result(c):
+        at = pl.ds(pl.multiple_of(c * rows, rows), rows)
+        return pltpu.make_async_copy(acc.at[at], sums_hbm.at[at], osem.at[c])
+
+    def step(now):
+        for k in range(plan.K + 2):
+            @pl.when(now == work.small_at + k * work.lag)
+            def _():
+                if k > 0:
+                    small_copy(plan, small, got, s2sem, r2sem, k - 1).wait()
+                    small[...] = small[...] + got[k - 1]
+                if k <= plan.K:
+                    small_copy(plan, small, got, s2sem, r2sem, k).start()
+        tick(plan, work.chunks, acc, recv, ssem, rsem, free, now, lambda c: to_result(c).start())
+
+    step(t)
+
+    i = t - work.first_tile
+
+    @pl.when((i >= 0) & (i < work.tiles))
+    def _():
+        back_tile(i, a_ref, b_ref, zc_ref, fc_ref, ic_ref, s_ref, gs_ref, xp_ref, gres_ref, wg_ref,
+                  gain_ref, gin_ref, gm, gmt, ggb, ggain, state, perm)
+
+    @pl.when(t == work.steps - 1)
+    def _():
+        def drain(now, _):
+            step(now)
+            return 0
+
+        lax.fori_loop(work.steps, work.ticks, drain, 0)
+        small_ref[...] = small[...]
+
+        def wait(c, _):
+            to_result(c).wait()
+            return 0
+
+        lax.fori_loop(0, work.chunks, wait, 0)
+
+
+def last_kernel(work, sizes, pieces, small_ref, gin, sums, gin_o, down_o, up_o, out_o, gates_o, *rest):
+    vecs, (gin_v, sums_v, insem, sem) = rest[:-4], rest[-4:]
+    rows = work.rows
     d = rows * work.halves
-
-    def to_result(c, action):
-        src = acc.at[pl.ds(pl.multiple_of(c * rows, rows), rows)]
-
-        def case(first, count, ref, tall):
-            @pl.when((c >= first) & (c < first + count))
-            def _():
-                k = c - first
-                if tall:
-                    dst = ref.at[pl.ds(pl.multiple_of(k * rows, rows), rows)]
-                else:
-                    dst = ref.at[
-                        pl.ds(pl.multiple_of((k % work.halves) * rows, rows), rows),
-                        pl.ds(pl.multiple_of((k // work.halves) * d, d), d),
-                    ]
-                action(pltpu.make_async_copy(src, dst, osem.at[c]))
-
-        case(0, work.down, down_hbm, True)
-        case(work.at_up, work.up, up_hbm, False)
-        case(work.at_out, work.out, out_hbm, True)
-        case(work.at_gates, work.gates, gates_hbm, False)
-
-    tick(plan, work.chunks, acc, recv, ssem, rsem, free, t,
-         lambda c: to_result(c, lambda copy: copy.start()), work.lag)
-
-    i = t - work.first_tile
-
-    @pl.when((i >= 0) & (i < work.tiles))
-    def _():
-        back_tile(i, a_ref, b_ref, zc_ref, fc_ref, ic_ref, s_ref, gs_ref, xp_ref, gres_ref, wg_ref,
-                  gain_ref, gin_ref, gm, ggb, ggain, state, perm)
-
-    @pl.when(t == work.ticks - 1)
-    def _():
-        small_ref[...] = small[...]
-
-        def wait(c, _):
-            to_result(c, lambda copy: copy.wait())
-            return 0
-
-        lax.fori_loop(0, work.chunks, wait, 0)
+    step = gin.shape[1] // pieces
+    moves = []
+
+    def move(src, via, dst):
+        k = len(moves)
+        read = pltpu.make_async_copy(src, via, insem.at[k])
+        read.start()
+        moves.append((read, pltpu.make_async_copy(via, dst, sem.at[k])))
+
+    for k in range(pieces):
+        part = lambda ref: ref.at[:, pl.ds(k * step, step)]
+        move(part(gin), part(gin_v), part(gin_o))
+    for first, count, ref, tall in (
+        (0, work.down, down_o, True),
+        (work.at_up, work.up, up_o, False),
+        (work.at_out, work.out, out_o, True),
+        (work.at_gates, work.gates, gates_o, False),
+    ):
+        for k in range(count):
+            at = pl.ds((first + k) * rows, rows)
+            if tall:
+                dst = ref.at[pl.ds(k * rows, rows)]
+            else:
+                dst = ref.at[pl.ds(k % work.halves * rows, rows), pl.ds(k // work.halves * d, d)]
+            move(sums.at[at], sums_v.at[at], dst)
+    line = 0
+    for ref, n in zip(vecs, sizes):
+        for k in range(n // LANES):
+            ref[:, k * LANES : (k + 1) * LANES] = small_ref[line : line + 1, :]
+            line += 1
+    for read, write in moves:
+        read.wait()
+        write.start()
+    for _, write in moves:
+        write.wait()
 
 
 def full(shape):
@@ -628,8 +646,8 @@
     params = pltpu.CompilerParams(
         dimension_semantics=("arbitrary",), vmem_limit_bytes=56 << 20
     )
-    a, b, zc, fc, ic, xp, nt, prod, total = pl.pallas_call(
-        functools.partial(gates_kernel, piece),
+    a, b, zc, fc, ic, xp, nt, prod, enter = pl.pallas_call(
+        functools.partial(gates_kernel, piece, seq),
         grid=(grid,),
         in_specs=[
             pl.BlockSpec(memory_space=pltpu.SMEM), pl.BlockSpec(memory_space=pltpu.SMEM),
@@ -638,11 +656,12 @@
         out_specs=[rows(hid)] * 5 + [rows(d), turned, held((SUB, hid)), held((SUB, hid))],
         out_shape=[sds((tok, hid), F32)] * 3 + [sds((tok, hid), BF16)] * 2
         + [sds((tok, d), BF16), sds((d, tok), BF16), sds((SUB, hid), F32), sds((SUB, hid), F32)],
-        scratch_shapes=[pltpu.VMEM((d // 128, tile, 128), F32)],
-        compiler_params=params,
+        scratch_shapes=[pltpu.VMEM((d // 128, tile + SUB * SUB, 128), F32), pltpu.VMEM((SUB, hid), F32)]
+        + ends_scratch(seq, hid),
+        compiler_params=pltpu.CompilerParams(
+            dimension_semantics=("arbitrary",), collective_id=1, has_side_effects=True, vmem_limit_bytes=56 << 20
+        ),
     )(short_lengths, long_lengths, x, gain1, w_gates, gate_bias.reshape(1, 3 * hid))
-
-    enter = carry(seq, False, prod, total)
 
     outs = pl.pallas_call(
         mlp_kernel,
@@ -656,7 +675,7 @@
                    sds((2, halves, d // halves, tok), BF16), sds((tok, d), F32),
                    sds((tok, hid), F32), sds((SUB, piece, d), BF16),
                    sds((SUB, hid), F32), sds((SUB, d), F32), sds((SUB, ff), F32), sds((SUB, d), F32), sds((SUB, d), F32)],
-        scratch_shapes=[pltpu.VMEM((SUB, hid), F32), pltpu.VMEM((SUB, hid), F32), pltpu.VMEM((d // 128, tile, 128), F32)],
+        scratch_shapes=[pltpu.VMEM((SUB, hid), F32), pltpu.VMEM((SUB, hid), F32), pltpu.VMEM((d // 128, tile + SUB * SUB, 128), F32)],
         compiler_params=params,
     )(a, b, zc, xp, nt, dy, enter, w_out, w_up, w_down, out_bias.reshape(1, d), gain2, up_bias.reshape(1, ff),
       down_bias.reshape(1, d))
@@ -684,9 +703,9 @@
         gates = halves + jnp.clip(t - work.at_gates, 0, work.gates - 1) % halves
         return (jnp.where(t < work.at_out, up, gates), 0, 0)
 
-    gin, small, g_down, g_up, g_out, g_gates = pl.pallas_call(
+    gin, small, sums = pl.pallas_call(
         functools.partial(sum_kernel, work),
-        grid=(work.ticks,),
+        grid=(work.steps,),
         in_specs=[full((SUB, hid)), full((SUB, hid)), full((SUB, d)), full((SUB, ff)), full((SUB, d)), full((SUB, d)),
                   full((1, d)), full((d, 3 * hid)),
                   pl.BlockSpec((tok, work.rows), acts_at),
@@ -694,42 +713,46 @@
                   pl.BlockSpec((1, work.rows, tok), turned_at),
                   pl.BlockSpec((tok, d), lambda t: (0, jnp.clip(t - work.at_up, 0, work.up - 1) // halves))]
         + [btile(hid)] * 7 + [btile(d)] * 2,
-        out_specs=[pl.BlockSpec((SUB, bsteps, d), lambda t: (0, at_tile(t), 0)), held((lines, LANES))] + [any_space] * 4,
-        out_shape=[sds((SUB, piece, d), F32), sds((lines, LANES), F32), sds((ff, d), F32), sds((d, ff), F32),
-                   sds((hid, d), F32), sds((d, 3 * hid), F32)],
+        out_specs=[pl.BlockSpec((SUB, bsteps, d), lambda t: (0, at_tile(t), 0)), held((lines, LANES)), any_space],
+        out_shape=[sds((SUB, piece, d), F32), sds((lines, LANES), F32), sds((work.chunks * work.rows, d), F32)],
         scratch_shapes=[
             pltpu.VMEM((work.chunks * work.rows, d), F32),
             pltpu.VMEM((slots, plan.recv_rows, d), F32),
             pltpu.VMEM((3 * hid // d, tok, d), BF16),
+            pltpu.VMEM((back, 3 * hid), BF16),
             pltpu.VMEM((SUB, hid), F32),
             pltpu.VMEM((SUB, 3 * hid), F32),
             pltpu.VMEM((SUB, d), F32),
-            pltpu.VMEM((d // 128, back, 128), F32),
+            pltpu.VMEM((d // 128, back + SUB * SUB, 128), F32),
             pltpu.VMEM((lines, LANES), F32),
             pltpu.VMEM((plan.K + 1, lines, LANES), F32),
-            pltpu.VMEM((SUB, hid), F32),
-            pltpu.VMEM((seq - 1, SUB, hid), F32),
+            *ends_scratch(seq, hid)[:2],
             pltpu.SemaphoreType.DMA((slots, plan.stages)),
             pltpu.SemaphoreType.DMA((slots, plan.stages)),
             pltpu.SemaphoreType.REGULAR((slots, plan.K + 1)),
             pltpu.SemaphoreType.DMA((work.chunks,)),
             pltpu.SemaphoreType.DMA((plan.K + 1,)),
             pltpu.SemaphoreType.DMA((plan.K + 1,)),
-            pltpu.SemaphoreType.DMA((seq - 1,)),
-            pltpu.SemaphoreType.DMA((seq - 1,)),
+            *ends_scratch(seq, hid)[2:],
         ],
         compiler_params=pltpu.CompilerParams(
             dimension_semantics=("arbitrary",), collective_id=0, has_side_effects=True, vmem_limit_bytes=62 << 20
         ),
     )(prod, mu, gdb, gub, ggain2, gob, gain1, w_gates, acts, pairs, turns, gu,
       a, b, zc, fc, ic, s, gs, xp, gres)
-    small = small.reshape(-1)
-    vecs = []
-    at = 0
-    for n in (d, 3 * hid, d, d, ff, d):
-        vecs.append(small[at : at + n])
-        at += n
-    ggain1, ggb, gob, ggain2, gub, gdb = vecs
+    sizes = (d, 3 * hid, d, d, ff, d)
+    vmem = pl.BlockSpec(memory_space=pltpu.VMEM)
+    gin, g_down, g_up, g_out, g_gates, *vecs = pl.pallas_call(
+        functools.partial(last_kernel, work, sizes, grid),
+        in_specs=[vmem, any_space, any_space],
+        out_specs=[any_space] * 5 + [vmem] * 6,
+        out_shape=[sds(gin.shape, F32), sds((ff, d), F32), sds((d, ff), F32), sds((hid, d), F32), sds((d, 3 * hid), F32)]
+        + [sds((1, n), F32) for n in sizes],
+        scratch_shapes=[pltpu.VMEM(gin.shape, F32), pltpu.VMEM(sums.shape, F32),
+                        pltpu.SemaphoreType.DMA((grid + work.chunks,)), pltpu.SemaphoreType.DMA((grid + work.chunks,))],
+        compiler_params=pltpu.CompilerParams(vmem_limit_bytes=62 << 20),
+    )(small, gin, sums)
+    ggain1, ggb, gob, ggain2, gub, gdb = [v.reshape(-1) for v in vecs]
     return (result.reshape(inputs.shape), gin.reshape(inputs.shape), ggain1, g_gates, ggb, g_out, gob,
             ggain2, g_up, gub, g_down, gdb)
 

time: 273 us -> 253 us (0.927)
  local copies, waits for them, and re-layouts: 23.7 us -> 1.34 us
    unnamed x21 -> x1, local copies, waits for them, and re-layouts: 22.3 us -> 1.34 us
    pallas_call x3, Pallas kernels: 196 us -> 209 us  [the longest x1 167 us: per_device(): pl.pallas_call(functools.partial(sum_kernel, work), grid=(work.steps,), i...]
    pallas_call x1, Pallas kernels: 53 us -> 41.5 us  [per_device(): pl.pallas_call(mlp_kernel, grid=(grid,), in_specs=[rows(hid)] * 3 + [rows...]
where the time goes in v3:
time: 253 us
  Pallas kernels  251 us (99%)
    pallas_call x1, Pallas kernels, per_device(): pl.pallas_call(functools.partial(sum_kernel, work), grid=(work.steps,), i...  167 us
    pallas_call x1, Pallas kernels, per_device(): pl.pallas_call(mlp_kernel, grid=(grid,), in_specs=[rows(hid)] * 3 + [rows...  41.5 us
    pallas_call x1, Pallas kernels, per_device(): pl.pallas_call(functools.partial(gates_kernel, piece, seq), grid=(grid,),...  25.6 us
    pallas_call x1, Pallas kernels, per_device(): pl.pallas_call(functools.partial(last_kernel, work, sizes, grid), in_spec...  16.4 us

profile of v3, /device:TPU:0, one launch (start us, length us, event | category | flops | bytes accessed | tf_op | source)
XLA Modules:
  0.0 252.8 jit_solution(12711705098762559870)
XLA Ops:
  0.6 1.3 copy.26.long_ref
  2.0 25.6 %shard_map.229 = (f32[2048,1024]{1,0:T(8,128)}, f32[2048,1024]{1,0:T(8,128)}, f32[2048,1024]{1,0:T(8,128)}, bf16[2048,1024]{1,0:T(8,128)(2,1)}, bf16[2048,1024]{...) custom-call(s32[4,4]{1,0:T(4,128)} %short_ref.1, ...), custom_call_target="tpu_custom_call" | custom-call | tf_op jit(solution)/shard_map/pallas_call | solution.py:649
  27.6 41.5 %shard_map.230 = (f32[2048,1024]{1,0:T(8,128)}, bf16[2048,3072]{1,0:T(8,128)(2,1)}, bf16[2048,2048]{1,0:T(8,128)(2,1)}, bf16[2,2048,512]{2,1,0:T(8,128)(2,1)}, b...) custom-call(f32[2048,1024]{1,0:T(8,128)} %get-tuple-element.48.a_ref, ...), custom_call_target="tpu_custom_call" | custom-call | tf_op jit(solution)/shard_map/pallas_call | solution.py:666
  69.1 167.3 %shard_map.231 = (f32[8,256,512]{2,1,0:T(8,128)}, f32[32,256]{1,0:T(8,128)}, f32[8192,512]{1,0:T(8,128)}) custom-call(f32[8,1024]{1,0:T(8,128)} %get-tuple-element.55.prod_ref, f32[8,1024]{1,0:T(8,128)} %get-tuple-element.56.mu_ref, f32[8,512]{1,0:T(8,128)} %get-tuple-element.57.gdb_ref, f32[8,2048]{1,0:T(8,128)} %get-tuple-element.58.gub_ref, ...), custom_call_target="tpu_custom_call" | custom-call | tf_op jit(solution)/shard_map/pallas_call | solution.py:706
  236.4 16.4 %shard_map.232 = (f32[8,256,512]{2,1,0:T(8,128)}, f32[2048,512]{1,0:T(8,128)}, f32[512,2048]{1,0:T(8,128)}, f32[1024,512]{1,0:T(8,128)}, f32[512,3072]{1,0:T(8,1...) custom-call(f32[32,256]{1,0:T(8,128)} %get-tuple-element.70.small_re, ...), custom_call_target="tpu_custom_call" | custom-call | tf_op jit(solution)/shard_map/pallas_call | solution.py:745

commit v4 on v3

--- a/solution.py
+++ b/solution.py
@@ -155,9 +155,9 @@
         begins = begins | (pos == jnp.where(short, at, -1))
         at = at + short_ref[srow, k]
     at = jnp.int32(0)
-    for k in range(long_ref.shape[1]):
+    for k in range(long_ref.shape[0]):
         begins = begins | (pos == jnp.where(short, -1, at))
-        at = at + long_ref[lrow, k]
+        at = at + long_ref[k, lrow]
     keep = jnp.where(begins, 0.0, 1.0).astype(F32)
 
     @pl.when(i == 0)
@@ -215,9 +215,9 @@
 def mlp_kernel(
     a_ref, b_ref, zc_ref, xp_ref, nt_ref, dy_ref, carry_ref, wo_ref, wu_ref, wd_ref,
     obias_ref, gain_ref, ubias_ref, dbias_ref,
-    s_ref, acts_ref, gu_ref, rows_ref, turned_ref, gres_ref, gs_ref, result_ref,
+    gate_ref, slant_ref, acts_ref, gu_ref, rows_ref, turned_ref, gres_ref, result_ref,
     mu_ref, gdb_ref, gub_ref, ggain_ref, gob_ref,
-    state, prod, perm,
+    state, prod, perm, s_ref,
 ):
     i = pl.program_id(0)
     steps = dy_ref.shape[1]
@@ -236,6 +236,8 @@
         s_ref[sl, :] = st
     state[...] = st
     sb = s_ref[...].astype(BF16)
+    gate_ref[...] = b_ref[...].astype(BF16)
+    slant_ref[...] = (b_ref[...] * (s_ref[...] - zc_ref[...])).astype(BF16)
     ff = wu_ref.shape[1]
     acts_ref[:, ff:] = sb
     source = xp_ref[...].astype(F32)
@@ -275,7 +277,6 @@
     gob_ref[...] += fold_rows(gr.astype(F32))
     rows_ref[1] = gr
     gs = dot_t(gr, wo_ref[...])
-    gs_ref[...] = gs
     pr = prod[...]
     mu = mu_ref[...]
     for r in range(steps):
@@ -301,7 +302,7 @@
     def __init__(self, seq, batch, rows):
         sb = [("seq", w) for w in bits_of(seq)]
         bb = [("batch", w) for w in bits_of(batch)][1:]
-        self.orders = [sb + bb, sb[::-1] + bb, bb[:1] + sb + bb[1:], sb + bb, sb[::-1] + bb, bb[:1] + sb[::-1] + bb[1:]]
+        self.orders = [sb + bb, sb[::-1] + bb, bb[:1] + sb + bb[1:]]
         self.K = len(sb) + len(bb)
         self.rows = rows
         self.sizes = [rows]
@@ -431,14 +432,14 @@
         self.plan = Plan(seq, batch, rows)
         self.lag = lag
         self.tiles = tiles
-        self.first_tile = 2
+        self.first_tile = max(2, min(6, self.at_gates - tiles))
         self.small_at = max(self.first_tile + tiles, self.at_gates)
         self.ticks = max(self.chunks + self.plan.begins[-1], self.small_at + lag * (self.plan.K + 1)) + 1
         self.steps = max(self.chunks, self.small_at) + 1
         self.seq = seq
 
 
-def back_tile(i, a_ref, b_ref, zc_ref, fc_ref, ic_ref, s_ref, gs_ref, xp_ref, gres_ref, wg_ref, gain_ref,
+def back_tile(i, a_ref, gate_ref, slant_ref, fc_ref, ic_ref, gr_ref, xp_ref, gres_ref, wg_ref, wo_ref, gain_ref,
               gin_ref, gm, gmt, ggb, ggain, state, perm):
     steps = gin_ref.shape[1]
     rows = steps * SUB
@@ -447,16 +448,17 @@
     at = pl.ds(pl.multiple_of(gm.shape[1] - (i + 1) * rows, rows), rows)
     for j in range(hid // LANES):
         here = slice(j * LANES, (j + 1) * LANES)
+        gs = dot_t(gr_ref[0], wo_ref[here, :])
         mu = state[:, here]
         lams = [None] * steps
         for r in range(steps - 1, -1, -1):
             sl = slice(r * SUB, (r + 1) * SUB)
-            lams[r] = gs_ref[sl, here] + mu
+            lams[r] = gs[sl] + mu
             mu = a_ref[sl, here] * lams[r]
         state[:, here] = mu
         lam = jnp.concatenate(lams, axis=0)
-        gzc = lam * b_ref[:, here]
-        big = gzc * (s_ref[:, here] - zc_ref[:, here])
+        gzc = lam * gate_ref[:, here].astype(F32)
+        big = lam * slant_ref[:, here].astype(F32)
         parts = (
             (big * fc_ref[:, here].astype(F32)).astype(BF16),
             (-big * ic_ref[:, here].astype(F32)).astype(BF16),
@@ -481,9 +483,9 @@
 
 def sum_kernel(
     work,
-    prod_ref, mu_ref, gdb_ref, gub_ref, ggain2_ref, gob_ref, gain_ref, wg_ref,
+    prod_ref, mu_ref, gdb_ref, gub_ref, ggain2_ref, gob_ref, gain_ref, wg_ref, wo_ref,
     acts_ref, rows_ref, turned_ref, gu_ref,
-    a_ref, b_ref, zc_ref, fc_ref, ic_ref, s_ref, gs_ref, xp_ref, gres_ref,
+    a_ref, gate_ref, slant_ref, fc_ref, ic_ref, gr_ref, xp_ref, gres_ref,
     gin_ref, small_ref, sums_hbm,
     acc, recv, gm, gmt, state, ggb, ggain, perm, small, got, mine, theirs,
     ssem, rsem, free, osem, s2sem, r2sem, csem, crsem,
@@ -558,7 +560,7 @@
 
     @pl.when((i >= 0) & (i < work.tiles))
     def _():
-        back_tile(i, a_ref, b_ref, zc_ref, fc_ref, ic_ref, s_ref, gs_ref, xp_ref, gres_ref, wg_ref,
+        back_tile(i, a_ref, gate_ref, slant_ref, fc_ref, ic_ref, gr_ref, xp_ref, gres_ref, wg_ref, wo_ref,
                   gain_ref, gin_ref, gm, gmt, ggb, ggain, state, perm)
 
     @pl.when(t == work.steps - 1)
@@ -627,7 +629,7 @@
 
 
 def per_device(seq, batch, inputs, cotangent, short_lengths, long_lengths, norm_gain, w_gates, gate_bias, w_out,
-               out_bias, mlp_gain, w_up, up_bias, w_down, down_bias, tile=256, back=128):
+               out_bias, mlp_gain, w_up, up_bias, w_down, down_bias, tile=256, back=256):
     tok, d = inputs.shape[1:]
     hid = w_out.shape[0]
     ff = w_up.shape[1]
@@ -661,25 +663,26 @@
         compiler_params=pltpu.CompilerParams(
             dimension_semantics=("arbitrary",), collective_id=1, has_side_effects=True, vmem_limit_bytes=56 << 20
         ),
-    )(short_lengths, long_lengths, x, gain1, w_gates, gate_bias.reshape(1, 3 * hid))
+    )(short_lengths, long_lengths.T, x, gain1, w_gates, gate_bias.reshape(1, 3 * hid))
 
     outs = pl.pallas_call(
         mlp_kernel,
         grid=(grid,),
         in_specs=[rows(hid)] * 3 + [rows(d), turned, natural, full((SUB, hid)), full((hid, d)), full((d, ff)), full((ff, d)),
                   full((1, d)), full((1, d)), full((1, ff)), full((1, d))],
-        out_specs=[rows(hid), rows(ff + hid), rows(ff), pl.BlockSpec((2, tile, d), lambda i: (0, i, 0)),
-                   pl.BlockSpec((2, halves, d // halves, tile), lambda i: (0, 0, 0, i)), rows(d), rows(hid), natural,
+        out_specs=[rows(hid), rows(hid), rows(ff + hid), rows(ff), pl.BlockSpec((2, tile, d), lambda i: (0, i, 0)),
+                   pl.BlockSpec((2, halves, d // halves, tile), lambda i: (0, 0, 0, i)), rows(d), natural,
                    held((SUB, hid)), held((SUB, d)), held((SUB, ff)), held((SUB, d)), held((SUB, d))],
-        out_shape=[sds((tok, hid), F32), sds((tok, ff + hid), BF16), sds((tok, ff), BF16), sds((2, tok, d), BF16),
+        out_shape=[sds((tok, hid), BF16), sds((tok, hid), BF16), sds((tok, ff + hid), BF16), sds((tok, ff), BF16), sds((2, tok, d), BF16),
                    sds((2, halves, d // halves, tok), BF16), sds((tok, d), F32),
-                   sds((tok, hid), F32), sds((SUB, piece, d), BF16),
+                   sds((SUB, piece, d), BF16),
                    sds((SUB, hid), F32), sds((SUB, d), F32), sds((SUB, ff), F32), sds((SUB, d), F32), sds((SUB, d), F32)],
-        scratch_shapes=[pltpu.VMEM((SUB, hid), F32), pltpu.VMEM((SUB, hid), F32), pltpu.VMEM((d // 128, tile + SUB * SUB, 128), F32)],
+        scratch_shapes=[pltpu.VMEM((SUB, hid), F32), pltpu.VMEM((SUB, hid), F32), pltpu.VMEM((d // 128, tile + SUB * SUB, 128), F32),
+                        pltpu.VMEM((tile, hid), F32)],
         compiler_params=params,
     )(a, b, zc, xp, nt, dy, enter, w_out, w_up, w_down, out_bias.reshape(1, d), gain2, up_bias.reshape(1, ff),
       down_bias.reshape(1, d))
-    s, acts, gu, pairs, turns, gres, gs, result, mu, gdb, gub, ggain2, gob = outs
+    gate, slant, acts, gu, pairs, turns, gres, result, mu, gdb, gub, ggain2, gob = outs
 
     turns = turns.reshape(2 * halves, d // halves, tok)
     work = Work(d, hid, ff, d // halves, tok // back, LAG, seq, batch)
@@ -707,12 +710,12 @@
         functools.partial(sum_kernel, work),
         grid=(work.steps,),
         in_specs=[full((SUB, hid)), full((SUB, hid)), full((SUB, d)), full((SUB, ff)), full((SUB, d)), full((SUB, d)),
-                  full((1, d)), full((d, 3 * hid)),
+                  full((1, d)), full((d, 3 * hid)), full((hid, d)),
                   pl.BlockSpec((tok, work.rows), acts_at),
-                  pl.BlockSpec((1, tok, d), lambda t: (jnp.where(t < work.at_up, 0, 1), 0, 0)),
+                  pl.BlockSpec((1, tok, d), lambda t: (jnp.where(t < work.at_up, 0, 1), 0, 0), pipeline_mode=pl.Buffered(1)),
                   pl.BlockSpec((1, work.rows, tok), turned_at),
                   pl.BlockSpec((tok, d), lambda t: (0, jnp.clip(t - work.at_up, 0, work.up - 1) // halves))]
-        + [btile(hid)] * 7 + [btile(d)] * 2,
+        + [btile(hid)] * 5 + [pl.BlockSpec((1, back, d), lambda t: (1, at_tile(t), 0))] + [btile(d)] * 2,
         out_specs=[pl.BlockSpec((SUB, bsteps, d), lambda t: (0, at_tile(t), 0)), held((lines, LANES)), any_space],
         out_shape=[sds((SUB, piece, d), F32), sds((lines, LANES), F32), sds((work.chunks * work.rows, d), F32)],
         scratch_shapes=[
@@ -738,8 +741,8 @@
         compiler_params=pltpu.CompilerParams(
             dimension_semantics=("arbitrary",), collective_id=0, has_side_effects=True, vmem_limit_bytes=62 << 20
         ),
-    )(prod, mu, gdb, gub, ggain2, gob, gain1, w_gates, acts, pairs, turns, gu,
-      a, b, zc, fc, ic, s, gs, xp, gres)
+    )(prod, mu, gdb, gub, ggain2, gob, gain1, w_gates, w_out, acts, pairs, turns, gu,
+      a, gate, slant, fc, ic, pairs, xp, gres)
     sizes = (d, 3 * hid, d, d, ff, d)
     vmem = pl.BlockSpec(memory_space=pltpu.VMEM)
     gin, g_down, g_up, g_out, g_gates, *vecs = pl.pallas_call(

time: 253 us -> 245 us (0.968)
  Pallas kernels: 251 us -> 244 us
    pallas_call x1, Pallas kernels: 167 us -> 159 us  [per_device(): pl.pallas_call(functools.partial(sum_kernel, work), grid=(work.steps,), i...]
where the time goes in v4:
time: 245 us; the launch traced here: 244 us
  Pallas kernels  244 us (100%)
    pallas_call x1, Pallas kernels, per_device(): pl.pallas_call(functools.partial(sum_kernel, work), grid=(work.steps,), i...  159 us
    pallas_call x1, Pallas kernels, per_device(): pl.pallas_call(mlp_kernel, grid=(grid,), in_specs=[rows(hid)] * 3 + [rows...  42.3 us
    pallas_call x1, Pallas kernels, per_device(): pl.pallas_call(functools.partial(gates_kernel, piece, seq), grid=(grid,),...  25.7 us
    pallas_call x1, Pallas kernels, per_device(): pl.pallas_call(functools.partial(last_kernel, work, sizes, grid), in_spec...  16.4 us

profile of v4, /device:TPU:0, one launch (start us, length us, event | category | flops | bytes accessed | tf_op | source)
XLA Modules:
  0.0 244.3 jit_solution(327157646849128885)
XLA Ops:
  0.6 25.7 %shard_map.229 = (f32[2048,1024]{1,0:T(8,128)}, f32[2048,1024]{1,0:T(8,128)}, f32[2048,1024]{1,0:T(8,128)}, bf16[2048,1024]{1,0:T(8,128)(2,1)}, bf16[2048,1024]{...) custom-call(s32[4,4]{1,0:T(4,128)} %short_ref.1, ...), custom_call_target="tpu_custom_call" | custom-call | tf_op jit(solution)/shard_map/pallas_call | solution.py:651
  26.3 42.3 %shard_map.230 = (bf16[2048,1024]{1,0:T(8,128)(2,1)}, bf16[2048,1024]{1,0:T(8,128)(2,1)}, bf16[2048,3072]{1,0:T(8,128)(2,1)}, bf16[2048,2048]{1,0:T(8,128)(2,1)}...) custom-call(f32[2048,1024]{1,0:T(8,128)} %get-tuple-element.48.a_ref, ...), custom_call_target="tpu_custom_call" | custom-call | tf_op jit(solution)/shard_map/pallas_call | solution.py:668
  68.6 159.3 %shard_map.231 = (f32[8,256,512]{2,1,0:T(8,128)}, f32[32,256]{1,0:T(8,128)}, f32[8192,512]{1,0:T(8,128)}) custom-call(f32[8,1024]{1,0:T(8,128)} %get-tuple-element.55.prod_ref, f32[8,1024]{1,0:T(8,128)} %get-tuple-element.56.mu_ref, f32[8,512]{1,0:T(8,128)} %get-tuple-element.57.gdb_ref, f32[8,2048]{1,0:T(8,128)} %get-tuple-element.58.gub_ref, ...), custom_call_target="tpu_custom_call" | custom-call | tf_op jit(solution)/shard_map/pallas_call | solution.py:709
  227.9 16.4 %shard_map.232 = (f32[8,256,512]{2,1,0:T(8,128)}, f32[2048,512]{1,0:T(8,128)}, f32[512,2048]{1,0:T(8,128)}, f32[1024,512]{1,0:T(8,128)}, f32[512,3072]{1,0:T(8,1...) custom-call(f32[32,256]{1,0:T(8,128)} %get-tuple-element.70.small_re, ...), custom_call_target="tpu_custom_call" | custom-call | tf_op jit(solution)/shard_map/pallas_call | solution.py:748

commit v5 on v4

--- a/solution.py
+++ b/solution.py
@@ -295,7 +295,7 @@
     return out
 
 def stage_ticks(j, stages):
-    return LAG
+    return 2 if j in (0, stages - 1) else LAG
 
 
 class Plan:
@@ -497,17 +497,16 @@
     b = lax.axis_index("batch")
     ends = Ends(work.seq, mine, theirs, csem, crsem)
 
+    who = [(s, flip(b, 1))] + [(o, b) for o in ends.others]
+    who += [(s, flip(b, w)) for axis, w in plan.orders[0] if axis == "batch"]
+
     @pl.when(t == 0)
     def _():
-        who = [(s, flip(b, 1))] + [(o, b) for o in ends.others]
-        who += [(s, flip(b, w)) for axis, w in plan.orders[0] if axis == "batch"]
         bar = pltpu.get_barrier_semaphore()
         for p in who:
             pl.semaphore_signal(bar, inc=1, device_id=p, device_id_type=MESH)
         ggb[...] = jnp.zeros_like(ggb)
         ggain[...] = jnp.zeros_like(ggain)
-        pl.semaphore_wait(bar, len(who))
-        ends.send(prod_ref, mu_ref, True)
 
     @pl.when(t == work.first_tile)
     def _():
@@ -527,6 +526,11 @@
     @pl.when((t >= work.at_gates) & (t < work.chunks))
     def _():
         put(dot(turned_ref[0], gm[(t - work.at_gates) // work.halves]))
+
+    @pl.when(t == 0)
+    def _():
+        pl.semaphore_wait(pltpu.get_barrier_semaphore(), len(who))
+        ends.send(prod_ref, mu_ref, True)
 
     @pl.when(t == work.small_at)
     def _():

time: 245 us -> 244 us (level)
  no operation moved by 1% of the time
where the time goes in v5:
time: 244 us; the launch traced here: 243 us
  Pallas kernels  243 us (100%)
    pallas_call x1, Pallas kernels, per_device(): pl.pallas_call(functools.partial(sum_kernel, work), grid=(work.steps,), i...  158 us
    pallas_call x1, Pallas kernels, per_device(): pl.pallas_call(mlp_kernel, grid=(grid,), in_specs=[rows(hid)] * 3 + [rows...  42.3 us
    pallas_call x1, Pallas kernels, per_device(): pl.pallas_call(functools.partial(gates_kernel, piece, seq), grid=(grid,),...  25.7 us
    pallas_call x1, Pallas kernels, per_device(): pl.pallas_call(functools.partial(last_kernel, work, sizes, grid), in_spec...  16.4 us

profile of v5, /device:TPU:0, one launch (start us, length us, event | category | flops | bytes accessed | tf_op | source)
XLA Modules:
  0.0 243.4 jit_solution(9993385415125288187)
XLA Ops:
  0.6 25.7 %shard_map.229 = (f32[2048,1024]{1,0:T(8,128)}, f32[2048,1024]{1,0:T(8,128)}, f32[2048,1024]{1,0:T(8,128)}, bf16[2048,1024]{1,0:T(8,128)(2,1)}, bf16[2048,1024]{...) custom-call(s32[4,4]{1,0:T(4,128)} %short_ref.1, ...), custom_call_target="tpu_custom_call" | custom-call | tf_op jit(solution)/shard_map/pallas_call | solution.py:655
  26.3 42.3 %shard_map.230 = (bf16[2048,1024]{1,0:T(8,128)(2,1)}, bf16[2048,1024]{1,0:T(8,128)(2,1)}, bf16[2048,3072]{1,0:T(8,128)(2,1)}, bf16[2048,2048]{1,0:T(8,128)(2,1)}...) custom-call(f32[2048,1024]{1,0:T(8,128)} %get-tuple-element.48.a_ref, ...), custom_call_target="tpu_custom_call" | custom-call | tf_op jit(solution)/shard_map/pallas_call | solution.py:672
  68.6 158.4 %shard_map.231 = (f32[8,256,512]{2,1,0:T(8,128)}, f32[32,256]{1,0:T(8,128)}, f32[8192,512]{1,0:T(8,128)}) custom-call(f32[8,1024]{1,0:T(8,128)} %get-tuple-element.55.prod_ref, f32[8,1024]{1,0:T(8,128)} %get-tuple-element.56.mu_ref, f32[8,512]{1,0:T(8,128)} %get-tuple-element.57.gdb_ref, f32[8,2048]{1,0:T(8,128)} %get-tuple-element.58.gub_ref, ...), custom_call_target="tpu_custom_call" | custom-call | tf_op jit(solution)/shard_map/pallas_call | solution.py:713
  227.0 16.4 %shard_map.232 = (f32[8,256,512]{2,1,0:T(8,128)}, f32[2048,512]{1,0:T(8,128)}, f32[512,2048]{1,0:T(8,128)}, f32[1024,512]{1,0:T(8,128)}, f32[512,3072]{1,0:T(8,1...) custom-call(f32[32,256]{1,0:T(8,128)} %get-tuple-element.70.small_re, ...), custom_call_target="tpu_custom_call" | custom-call | tf_op jit(solution)/shard_map/pallas_call | solution.py:752

commit v6 on v5

--- a/solution.py
+++ b/solution.py
@@ -97,8 +97,11 @@
         for c in range(SUB - 1, -1, -1) if reverse else range(SUB):
             prod = prod * prod_ref[c : c + 1, :]
             total = total * prod_ref[c : c + 1, :] + sum_ref[c : c + 1, :]
-        self.mine[0:1, :] = prod
-        self.mine[1:2, :] = total
+        half = SUB // 2
+        part = width // half
+        for k in range(half):
+            self.mine[k : k + 1, :] = prod[:, k * part : (k + 1) * part]
+            self.mine[half + k : half + k + 1, :] = total[:, k * part : (k + 1) * part]
         for copy in self.copies:
             copy.start()
 
@@ -110,7 +113,12 @@
         for owner in range(n - 1, 0, -1) if reverse else range(n - 1):
             back = lax.rem(self.at - owner + n, n)
             slot = jnp.where(back == 0, 0, back - 1)
-            new = self.theirs[slot, 0:1, :] * now + self.theirs[slot, 1:2, :]
+            got = self.theirs[slot]
+            half = SUB // 2
+            prod, total = [
+                jnp.concatenate([got[k : k + 1] for k in range(f, f + half)], axis=1) for f in (0, half)
+            ]
+            new = prod * now + total
             now = jnp.where(owner > self.at if reverse else owner < self.at, new, now)
         for c in range(SUB - 1, -1, -1) if reverse else range(SUB):
             out_ref[c : c + 1, :] = now
@@ -119,8 +127,8 @@
 
 def ends_scratch(devices, width):
     return [
-        pltpu.VMEM((SUB, width), F32),
-        pltpu.VMEM((devices - 1, SUB, width), F32),
+        pltpu.VMEM((SUB, width * 2 // SUB), F32),
+        pltpu.VMEM((devices - 1, SUB, width * 2 // SUB), F32),
         pltpu.SemaphoreType.DMA((devices - 1,)),
         pltpu.SemaphoreType.DMA((devices - 1,)),
     ]

time: 244 us -> 244 us (level)
  no operation moved by 1% of the time
where the time goes in v6:
time: 244 us; the launch traced here: 243 us
  Pallas kernels  243 us (100%)
    pallas_call x1, Pallas kernels, per_device(): pl.pallas_call(functools.partial(sum_kernel, work), grid=(work.steps,), i...  159 us
    pallas_call x1, Pallas kernels, per_device(): pl.pallas_call(mlp_kernel, grid=(grid,), in_specs=[rows(hid)] * 3 + [rows...  42.3 us
    pallas_call x1, Pallas kernels, per_device(): pl.pallas_call(functools.partial(gates_kernel, piece, seq), grid=(grid,),...  25.4 us
    pallas_call x1, Pallas kernels, per_device(): pl.pallas_call(functools.partial(last_kernel, work, sizes, grid), in_spec...  16.4 us

profile of v6, /device:TPU:0, one launch (start us, length us, event | category | flops | bytes accessed | tf_op | source)
XLA Modules:
  0.0 243.3 jit_solution(13745704996148709773)
XLA Ops:
  0.6 25.4 %shard_map.229 = (f32[2048,1024]{1,0:T(8,128)}, f32[2048,1024]{1,0:T(8,128)}, f32[2048,1024]{1,0:T(8,128)}, bf16[2048,1024]{1,0:T(8,128)(2,1)}, bf16[2048,1024]{...) custom-call(s32[4,4]{1,0:T(4,128)} %short_ref.1, ...), custom_call_target="tpu_custom_call" | custom-call | tf_op jit(solution)/shard_map/pallas_call | solution.py:663
  26.1 42.3 %shard_map.230 = (bf16[2048,1024]{1,0:T(8,128)(2,1)}, bf16[2048,1024]{1,0:T(8,128)(2,1)}, bf16[2048,3072]{1,0:T(8,128)(2,1)}, bf16[2048,2048]{1,0:T(8,128)(2,1)}...) custom-call(f32[2048,1024]{1,0:T(8,128)} %get-tuple-element.48.a_ref, ...), custom_call_target="tpu_custom_call" | custom-call | tf_op jit(solution)/shard_map/pallas_call | solution.py:680
  68.3 158.5 %shard_map.231 = (f32[8,256,512]{2,1,0:T(8,128)}, f32[32,256]{1,0:T(8,128)}, f32[8192,512]{1,0:T(8,128)}) custom-call(f32[8,1024]{1,0:T(8,128)} %get-tuple-element.55.prod_ref, f32[8,1024]{1,0:T(8,128)} %get-tuple-element.56.mu_ref, f32[8,512]{1,0:T(8,128)} %get-tuple-element.57.gdb_ref, f32[8,2048]{1,0:T(8,128)} %get-tuple-element.58.gub_ref, ...), custom_call_target="tpu_custom_call" | custom-call | tf_op jit(solution)/shard_map/pallas_call | solution.py:721
  226.9 16.4 %shard_map.232 = (f32[8,256,512]{2,1,0:T(8,128)}, f32[2048,512]{1,0:T(8,128)}, f32[512,2048]{1,0:T(8,128)}, f32[1024,512]{1,0:T(8,128)}, f32[512,3072]{1,0:T(8,1...) custom-call(f32[32,256]{1,0:T(8,128)} %get-tuple-element.70.small_re, ...), custom_call_target="tpu_custom_call" | custom-call | tf_op jit(solution)/shard_map/pallas_call | solution.py:760
